TPU v7x, 256 devices: a whole 4x4x8 slice. The times are simulated.
256 devices in a mesh: head: 4 (over x), inner: 16 (over z, core), outer: 4 (over y).
Axes of the slice: x: 4, y: 4, z: 8, core: 2. Of those that a mesh axis runs over, the one named last changes fastest.
Arguments:
- queries: bfloat16 [8192, 64, 128], P(('outer', 'inner'), None, 'head'), may hold values from -6 to 6
- keys: bfloat16 [8192, 8, 128], P(('outer', 'inner'), None, 'head'), may hold values from -6 to 6
- values: bfloat16 [8192, 8, 128], P(('outer', 'inner'), None, 'head'), may hold values from -6 to 6
- grad_out: bfloat16 [8192, 64, 128], P(('outer', 'inner'), None, 'head'), may hold values from -6 to 6
- span_order: int32 [128], replicated, may hold values from 0 to 127, as said below
- doc_ids: int32 [8192], replicated, may hold values from 0 to 3, never falling along the last dimension, each value on 1 to 4096 neighbouring positions
Outputs:
- attn_out: bfloat16 [8192, 64, 128], P(('outer', 'inner'), 'head')
- query_grads: float32 [8192, 64, 128], P(('outer', 'inner'), 'head')
- key_grads: float32 [8192, 8, 128], P(('outer', 'inner'), 'head')
- value_grads: float32 [8192, 8, 128], P(('outer', 'inner'), 'head')
Inputs may be any that keep to these rules, and one draw needn't show every extreme that they name: `span_order`: stored span slots 2r and 2r+1 hold the spans c and 127 - c for some c; every span appears once. doc_ids never falls along the sequence.
All inputs are finite; a program needn't handle non-finite values.
Results may differ from a plain program's by a relative error of at most 0.025.
Values may be sent and summed in bfloat16 or wider, within the bound.
A program may use at most 64 MiB of HBM per device.

v0:
```python
import math

import jax
import jax.numpy as jnp
from jax import lax
from jax.sharding import PartitionSpec as P

NEG = -1e30


def from_behind(array, axis, by):
    devices = lax.axis_size(axis)
    return lax.ppermute(array, axis, [(i, (i + by) % devices) for i in range(devices)])


def token_meta(row_ids, span_order, doc_ids, span_rows):
    slot_index = row_ids // span_rows
    slot_ids = jnp.arange(span_order.shape[0], dtype=jnp.int32)
    span_ids = jnp.sum(
        jnp.where(slot_index[:, None] == slot_ids[None, :], span_order[None, :], 0), axis=1
    )
    position = span_ids * span_rows + row_ids % span_rows
    return (position, jnp.take(doc_ids, position))


def local(queries, keys, values, grad_out, span_order, doc_ids):
    query_tile, key_tile, value_tile, grad_tile = (
        lax.all_to_all(queries, "head", split_axis=1, concat_axis=2, tiled=True),
        lax.all_to_all(keys, "head", split_axis=1, concat_axis=2, tiled=True),
        lax.all_to_all(values, "head", split_axis=1, concat_axis=2, tiled=True),
        lax.all_to_all(grad_out, "head", split_axis=1, concat_axis=2, tiled=True),
    )
    block_rows = query_tile.shape[0]
    heads_local = query_tile.shape[1]
    head_dim = query_tile.shape[2]
    kv_local = key_tile.shape[1]
    group_size = heads_local // kv_local
    span_rows = block_rows // 2
    n_inner = lax.axis_size("inner")
    n_outer = lax.axis_size("outer")
    group_rows = n_inner * block_rows
    outer_pos = lax.axis_index("outer")
    inner_pos = lax.axis_index("inner")
    score_scale = 1.0 / math.sqrt(head_dim)
    kv_own = jnp.stack((key_tile, value_tile), 0)
    kv_prev = from_behind(kv_own, "outer", 1)
    cycle_own, cycle_prev = (
        lax.all_gather(kv_own, "inner", axis=1, tiled=True),
        lax.all_gather(kv_prev, "inner", axis=1, tiled=True),
    )
    window_kv = jnp.concatenate((cycle_own, cycle_prev), 1)
    block_iota = jnp.arange(block_rows, dtype=jnp.int32)
    group_iota = jnp.arange(group_rows, dtype=jnp.int32)
    query_rows = (outer_pos * n_inner + inner_pos) * block_rows + block_iota
    own_start = outer_pos * group_rows
    prev_start = (outer_pos + n_outer - 1) % n_outer * group_rows
    key_rows = jnp.concatenate((own_start + group_iota, prev_start + group_iota))
    query_pos, query_doc = token_meta(query_rows, span_order, doc_ids, span_rows)
    key_pos, key_doc = token_meta(key_rows, span_order, doc_ids, span_rows)
    query_four = query_tile.reshape(block_rows, kv_local, group_size, head_dim)
    grad_four = grad_tile.reshape(block_rows, kv_local, group_size, head_dim)
    num_blocks = 2 * n_inner

    def block_mask(index):
        block_pos = lax.dynamic_slice_in_dim(key_pos, index * block_rows, block_rows, 0)
        block_doc = lax.dynamic_slice_in_dim(key_doc, index * block_rows, block_rows, 0)
        return (block_pos[None, :] <= query_pos[:, None]) & (
            block_doc[None, :] == query_doc[:, None]
        )

    def block_scores(block_kv):
        return (
            jnp.einsum(
                "qcgd,kcd->qcgk", query_four, block_kv[0], preferred_element_type=jnp.float32
            )
            * score_scale
        )

    def forward_step(index, carried):
        tile_mask = block_mask(index)
        block_kv = lax.dynamic_slice_in_dim(window_kv, index * block_rows, block_rows, 1)
        row_max, row_sum, accum = carried
        scores = block_scores(block_kv)
        wide_mask = tile_mask[:, None, None, :]
        new_max = jnp.maximum(row_max, jnp.max(jnp.where(wide_mask, scores, NEG), axis=-1))
        factor = jnp.exp(row_max - new_max)
        probs = jnp.where(wide_mask, jnp.exp(scores - new_max[..., None]), 0.0)
        new_sum = factor * row_sum + jnp.sum(probs, axis=-1)
        update = jnp.einsum(
            "qcgk,kcd->qcgd",
            probs.astype(jnp.bfloat16),
            block_kv[1],
            preferred_element_type=jnp.float32,
        )
        return (new_max, new_sum, factor[..., None] * accum + update)

    start_max = jnp.full((block_rows, kv_local, group_size), NEG, jnp.float32)
    start_sum = jnp.zeros((block_rows, kv_local, group_size), jnp.float32)
    start_acc = jnp.zeros((block_rows, kv_local, group_size, head_dim), jnp.float32)
    row_max, row_sum, accum = lax.fori_loop(
        0, num_blocks, forward_step, (start_max, start_sum, start_acc)
    )
    attn_four = (accum / row_sum[..., None]).astype(jnp.bfloat16)
    log_total = row_max + jnp.log(row_sum)
    row_dot = jnp.sum(grad_four.astype(jnp.float32) * attn_four.astype(jnp.float32), axis=-1)

    def backward_step(index, carried):
        tile_mask = block_mask(index)
        block_kv = lax.dynamic_slice_in_dim(window_kv, index * block_rows, block_rows, 1)
        query_acc, grad_terms = carried
        scores = block_scores(block_kv)
        wide_mask = tile_mask[:, None, None, :]
        probs = jnp.where(wide_mask, jnp.exp(scores - log_total[..., None]), 0.0)
        value_part = jnp.einsum(
            "qcgk,qcgd->kcd",
            probs.astype(jnp.bfloat16),
            grad_four,
            preferred_element_type=jnp.float32,
        )
        prob_grads = jnp.einsum(
            "qcgd,kcd->qcgk", grad_four, block_kv[1], preferred_element_type=jnp.float32
        )
        score_grads = (probs * (prob_grads - row_dot[..., None])).astype(jnp.bfloat16)
        query_acc = (
            query_acc
            + jnp.einsum(
                "qcgk,kcd->qcgd", score_grads, block_kv[0], preferred_element_type=jnp.float32
            )
            * score_scale
        )
        key_part = (
            jnp.einsum(
                "qcgk,qcgd->kcd", score_grads, query_four, preferred_element_type=jnp.float32
            )
            * score_scale
        )
        grad_terms = lax.dynamic_update_slice_in_dim(
            grad_terms, jnp.stack((key_part, value_part), 0), index * block_rows, 1
        )
        return (query_acc, grad_terms)

    start_query = jnp.zeros((block_rows, kv_local, group_size, head_dim), jnp.float32)
    start_terms = jnp.zeros((2, 2 * group_rows, kv_local, head_dim), jnp.float32)
    query_acc, grad_terms = lax.fori_loop(0, num_blocks, backward_step, (start_query, start_terms))
    grad_split = grad_terms.reshape(2, 2, group_rows, kv_local, head_dim)
    summed = lax.psum_scatter(
        grad_split.astype(jnp.bfloat16), "inner", scatter_dimension=2, tiled=True
    ).astype(jnp.float32)
    returned = from_behind(summed[:, 1].astype(jnp.bfloat16), "outer", -1).astype(jnp.float32)
    key_grads = summed[0, 0] + returned[0]
    value_grads = summed[1, 0] + returned[1]
    attn_out = attn_four.reshape(block_rows, heads_local, head_dim)
    query_grads = query_acc.reshape(block_rows, heads_local, head_dim)
    return (attn_out, query_grads, key_grads, value_grads)


def solution(mesh):
    placed = (
        P(("outer", "inner"), None, "head"),
        P(("outer", "inner"), None, "head"),
        P(("outer", "inner"), None, "head"),
        P(("outer", "inner"), None, "head"),
        P(),
        P(),
    )
    return jax.shard_map(
        local,
        mesh=mesh,
        in_specs=placed,
        out_specs=(
            P(("outer", "inner"), "head", None),
            P(("outer", "inner"), "head", None),
            P(("outer", "inner"), "head", None),
            P(("outer", "inner"), "head", None),
        ),
        check_vma=False,
    )
```

profile of v0, /device:TPU:26, one launch (start us, length us, event | category | flops | bytes accessed | tf_op | source)
XLA Modules:
  0.0 490.8 jit_solution(16295775187894947868)
XLA Ops:
  7.2 9.0 %all_to_all.60 = bf16[128,8,32]{0,2,1:T(8,128)(2,1)S(1)} all-to-all(bf16[128,8,32]{0,2,1:T(8,128)(2,1)} %param.11), channel_id=1, replica_groups=mesh['head'=4,'inner'=16,'outer'=4] {'head'}, dimensions={1} | all-to-all | bytes 131072 | tf_op jit(solution)/shard_map/all_to_all | solution.py:29
  16.2 4.7 all-to-all-start.1
  20.9 4.2 all-to-all-done.1
  26.8 4.3 collective-permute-done
  31.8 4.9 %all-to-all-start.2 = ((bf16[128,64,32]{0,2,1:T(8,128)(2,1)}), bf16[128,64,32]{0,2,1:T(8,128)(2,1)S(1)}, u32[]{:S(2)}, u32[]{:S(2)}) async-start(bf16[128,64,32]{0,2,1:T(8,128)(2,1)} %param.10), calls=%async_computation.2 | async-start | bytes 1048576 | tf_op jit(solution)/shard_map/all_to_all | solution.py:28
  37.5 1.9 select_reduce_fusion.1
  40.8 23.0 %gather_fusion = s32[4096]{0:T(1024)S(1)} fusion(s32[8192]{0:T(1024)S(1)} %copy-done, s32[4096]{0:T(1024)S(1)} %broadcast_clamp_fusion), kind=kCustom, calls=%fused_computation | custom fusion | bytes 49152 | tf_op jit(solution)/shard_map/jit(_take)/gather | solution.py:23
  63.9 4.8 all-to-all-start.3
  70.9 4.4 all-to-all-done.3
  77.5 33.6 %all-gather.5.cloned.1.call-done = bf16[2,2048,2,128]{1,3,2,0:T(8,128)(2,1)} async-done(((bf16[2,128,2,128]{1,3,2,0:T(8,128)(2,1)}), bf16[2,2048,2,128]{1,3,2,0:T(8,128)(2,1)}) %all-gather.5.cloned.1.call-update) | async-done | bytes 2097168 | tf_op jit(solution)/shard_map/all_gather | solution.py:49
  111.1 4.7 pad_maximum_fusion
  115.8 6.3 %copy.73 = bf16[2,4096,2,128]{3,1,2,0:T(8,128)(2,1)} copy(bf16[2,4096,2,128]{1,3,2,0:T(8,128)(2,1)} %pad_maximum_fusion) | data formatting | bytes 8388608
  122.1 96.3 %while.34 = (s32[]{:T(128)}, f32[128,2,8]{0,2,1:T(8,128)S(1)}, f32[128,2,8]{0,2,1:T(8,128)S(1)}, f32[128,2,8,128]{0,3,2,1:T(8,128)S(1)}, s32[4096]{0:T(1024)S(1)...) while((s32[]{:T(128)}, f32[128,2,8]{0,2,1:T(8,128)S(1)}, ...), condition=%wide.region_5.6_spmd.clone, body=%wide.region_2.5_spmd.clone.sunk | while | flops 137422848 | bytes 6099183 | solution.py:100
  218.4 2.0 multiply_reduce_fusion
  220.5 2.5 broadcast_in_dim.160
  223.0 169.1 %while.35 = (s32[]{:T(128)}, f32[128,2,8,128]{0,3,2,1:T(8,128)S(1)}, bf16[2,4096,2,128]{3,1,2,0:T(8,128)(2,1)}, bf16[2,4096,2,128]{3,1,2,0:T(8,128)(2,1)}, s32[4...) while((s32[]{:T(128)}, ...), condition=%wide.region_8.9_spmd.clone, body=%wide.region_7.8_spmd.clone.sunk | while | flops 338542592 | bytes 9556229 | solution.py:144
  231.5 1.4 fusion.77
  236.7 1.4 fusion.77
  252.6 1.4 fusion.77
  257.9 1.4 fusion.77
  273.8 1.4 fusion.77
  284.4 1.4 fusion.77
  300.2 1.4 fusion.77
  342.6 1.4 fusion.77
  347.8 1.4 fusion.77
  353.1 1.4 fusion.77
  392.1 8.4 %copy.80 = bf16[2,4096,2,128]{3,2,1,0:T(2,128)(2,1)S(1)} copy(bf16[2,4096,2,128]{3,1,2,0:T(8,128)(2,1)} %get-tuple-element.379) | data formatting | bytes 8388608 | tf_op jit(solution)/shard_map/convert_element_type | solution.py:147
  400.5 5.1 %copy.100 = bf16[2,2,2048,2,128]{4,3,1,0,2:T(2,128)(2,1)} copy(bf16[2,2,2048,2,128]{4,3,2,1,0:T(2,128)(2,1)S(1)} %bitcast.176) | data formatting | bytes 8388608
  405.6 7.7 %reshape.396 = bf16[2048,1024]{1,0:T(8,128)(2,1)} reshape(bf16[2048,2,2,2,128]{4,3,2,1,0:T(2,128)(2,1)} %bitcast.177) | data formatting | bytes 8388608
  413.4 62.2 %reduce-scatter.5.cloned.1.call-done = bf16[128,1024]{1,0:T(8,128)(2,1)} async-done(((bf16[2048,1024]{1,0:T(8,128)(2,1)}), bf16[128,1024]{1,0:T(8,128)(2,1)}) %reduce-scatter.5.cloned.1.call-update) | async-done | bytes 262160
  479.2 1.4 copy.79
  480.5 2.8 collective-permute-done.1
  (612 shorter events, 261.5 us)
Async XLA Ops:
  7.2 32.5 %copy-start = (s32[8192]{0:T(1024)S(1)}, s32[8192]{0:T(1024)}, u32[]{:S(2)}) copy-start(s32[8192]{0:T(1024)} %param.15) | copy-start | bytes 98308
  16.2 8.9 %all-to-all-start.1 = ((bf16[128,8,32]{0,2,1:T(8,128)(2,1)}), bf16[128,8,32]{0,2,1:T(8,128)(2,1)S(1)}, u32[]{:S(2)}, u32[]{:S(2)}) async-start(bf16[128,8,32]{0,2,1:T(8,128)(2,1)} %param.12), calls=%async_computation.1 | async-start | bytes 131072 | tf_op jit(solution)/shard_map/all_to_all | solution.py:30
  20.9 56.6 %all-gather.3.cloned.1.call-start = ((), (), s32[]{:S(2)}) async-start(), calls=%async_computation.5 | async-start | bytes 2228224 | tf_op jit(solution)/shard_map/all_gather | solution.py:48
  25.8 85.3 %all-gather.5.cloned.1.call-start = ((), (), s32[]{:S(2)}) async-start(), calls=%async_computation.6 | async-start | bytes 2228224 | tf_op jit(solution)/shard_map/all_gather | solution.py:49
  25.8 5.3 %collective-permute-start = (bf16[2,128,2,128]{1,3,2,0:T(8,128)(2,1)}, bf16[2,128,2,128]{1,3,2,0:T(8,128)(2,1)S(1)}, u32[]{:S(2)}, u32[]{:S(2)}) collective-permute-start(bf16[2,128,2,128]{1,3,2,0:T(8,128)(2,1)} %pad_maximum_fusion.1), channel_id=1, source_target_pairs={{0,1},{1,2},{2,3},{3,0},{4,5},{5,6},{6,7},{7,4},{8,9},{9,10},{10,1... | collective-permute-start | bytes 393224 | tf_op jit(solution)/shard_map/ppermute | solution.py:13
  31.1 0.7 copy-start.2
  31.8 32.1 %all-to-all-start.2 = ((bf16[128,64,32]{0,2,1:T(8,128)(2,1)}), bf16[128,64,32]{0,2,1:T(8,128)(2,1)S(1)}, u32[]{:S(2)}, u32[]{:S(2)}) async-start(bf16[128,64,32]{0,2,1:T(8,128)(2,1)} %param.10), calls=%async_computation.2 | async-start | bytes 1048576 | tf_op jit(solution)/shard_map/all_to_all | solution.py:28
  63.9 11.4 %all-to-all-start.3 = ((bf16[128,64,32]{0,2,1:T(8,128)(2,1)}), bf16[128,64,32]{0,2,1:T(8,128)(2,1)S(1)}, u32[]{:S(2)}, u32[]{:S(2)}) async-start(bf16[128,64,32]{0,2,1:T(8,128)(2,1)} %param.13), calls=%async_computation.3 | async-start | bytes 1048576 | tf_op jit(solution)/shard_map/all_to_all | solution.py:31
  68.7 406.9 %reduce-scatter.5.cloned.1.call-start = ((), (), s32[]{:S(2)}) async-start(), calls=%async_computation.7 | async-start | bytes 4456448
  413.4 64.6 %copy-start.1 = (bf16[128,2,8,128]{0,3,2,1:T(8,128)(2,1)S(1)}, bf16[128,2,8,128]{0,3,2,1:T(8,128)(2,1)}, u32[]{:S(2)}) copy-start(bf16[128,2,8,128]{0,3,2,1:T(8,128)(2,1)} %get-tuple-element.603) | copy-start | bytes 1572868
  477.1 6.3 %collective-permute-start.1 = (bf16[2,128,2,128]{3,2,1,0:T(2,128)(2,1)S(1)}, bf16[2,128,2,128]{3,2,1,0:T(2,128)(2,1)S(1)}, u32[]{:S(2)}, u32[]{:S(2)}) collective-permute-start(bf16[2,128,2,128]{3,2,1,0:T(2,128)(2,1)S(1)} %slice_bitcast_fusion.3), channel_id=1, source_target_pairs={{0,3},{1,0},{2,1},{3,2},{4,7},{5,4},{6,5},{7,6},{8,11},{9,8},{10,9... | collective-permute-start | bytes 393224 | tf_op jit(solution)/shard_map/ppermute | solution.py:13
Sparse Core Ops, SparseCore 0:
  25.9 42.6 all-gather.2
  70.9 40.0 all-gather.4
  413.5 62.0 reduce-scatter.4
where the time goes:
time: 499 us; the launch traced here: 491 us
  matrix products  216 us (43%)
  waiting for transfers between devices  111 us (22%)
  local copies, waits for them, and re-layouts  72.8 us (15%)
  other arithmetic  47.5 us (10%)
  starting transfers between devices  16.4 us (3%)
  between operations  13.9 us (3%)
  blocking collectives  9 us (2%)
    dot_general x64, matrix products, block_scores(): jnp.einsum('qcgd,kcd->qcgk', query_four, block_kv[0], preferred_element_t...  75.7 us
    unnamed x4, waiting for transfers between devices  62.2 us
    dot_general x32, matrix products, backward_step(): jnp.einsum('qcgk,kcd->qcgd', score_grads, block_kv[0], preferred_element_...  43.6 us
    dot_general x32, matrix products, forward_step(): jnp.einsum('qcgk,kcd->qcgd', probs.astype(jnp.bfloat16), block_kv[1], pre...  41.6 us
    dot_general x32, matrix products, backward_step(): jnp.einsum('qcgd,kcd->qcgk', grad_four, block_kv[1], preferred_element_ty...  36.8 us
    all_gather x1, waiting for transfers between devices, local(): lax.all_gather(kv_prev, 'inner', axis=1, tiled=True)  33.6 us
    unnamed x13, local copies, waits for them, and re-layouts  24.8 us
    gather x2, local copies, waits for them, and re-layouts, token_meta(): return (position, jnp.take(doc_ids, position))  24.2 us
  transfers between devices with their start and end apart: 8, of which 6 were waited for; matrix products, arithmetic and copies ran while one was open for 7% of the time, Pallas kernels for 0%

commit v1 on v0

v1 whole, which is shorter than its diff:
```python
import functools
import math

import jax
import jax.numpy as jnp
from jax import lax
from jax.experimental import pallas as pl
from jax.experimental.pallas import tpu as pltpu
from jax.sharding import PartitionSpec as P

MESH = pl.DeviceIdType.MESH
ANY = pl.BlockSpec(memory_space=pl.ANY)
VMEM = pl.BlockSpec(memory_space=pltpu.VMEM)
SMEM = pl.BlockSpec(memory_space=pltpu.SMEM)
NEG = -1e30
FAR = 1 << 24
NX = 4
NY = 4
NZ = 8
HD = 128
ROWS = 128
SPAN = 64
GROUP = 8
SLOTS = 64
LANES = GROUP * SPAN
SCALE = 1.0 / math.sqrt(HD)
LOG2E = math.log2(math.e)
BF16 = jnp.bfloat16
F32 = jnp.float32


def place():
    inner = lax.axis_index("inner")
    return (
        lax.axis_index("head"),
        lax.axis_index("outer"),
        lax.div(inner, 2),
        lax.rem(inner, 2),
    )


def where_is(x, y, z, core):
    return {"head": x, "outer": y, "inner": z * 2 + core}


def greet(partners):
    barrier = pltpu.get_barrier_semaphore()
    for partner in partners:
        pl.semaphore_signal(barrier, inc=1, device_id=partner, device_id_type=MESH)
    pl.semaphore_wait(barrier, len(partners))


def send(src, dst, send_sem, recv_sem, partner):
    copy = pltpu.make_async_remote_copy(
        src_ref=src,
        dst_ref=dst,
        send_sem=send_sem,
        recv_sem=recv_sem,
        device_id=partner,
        device_id_type=MESH,
    )
    copy.start()
    return copy


def bring_kernel(
    q, k, v, g, q_out, g_out, kv_out,
    kv_in, kv_rows, own_sem, x_send, x_recv, y_sem, z_send, z_recv,
):
    x, y, z, core = place()
    peers = [(dx, dc) for dx in range(NX) for dc in range(2) if (dx, dc) != (0, 0)]

    def peer(dx, dc):
        return where_is(lax.rem(x + dx, NX), y, z, lax.rem(core + dc, 2))

    up = where_is(x, y, lax.rem(z + 1, NZ), core)
    down = where_is(x, y, lax.rem(z + NZ - 1, NZ), core)
    later = where_is(x, lax.rem(y + 1, NY), z, core)
    earlier = where_is(x, lax.rem(y + NY - 1, NY), z, core)
    greet([peer(*p) for p in peers] + [up, down, later, earlier])

    here = pl.ds(pl.multiple_of(x * 32, 32), 32)
    copies = []
    own = []
    for index, (dx, dc) in enumerate([(0, 0)] + peers):
        head = lax.rem(x + dx, NX) * 2 + lax.rem(core + dc, 2)
        for kind, src in enumerate((k, v)):
            dst = kv_in.at[kind, core, here]
            if index == 0:
                copy = pltpu.make_async_copy(src.at[head], dst, own_sem.at[kind])
                copy.start()
                own.append(copy)
            else:
                copies.append(
                    send(src.at[head], dst, x_send.at[kind, index], x_recv.at[kind, index], peer(dx, dc))
                )
    heads = pl.ds((x * 2 + core) * GROUP, GROUP)
    for kind, (src, dst) in enumerate(((q, q_out), (g, g_out))):
        copy = pltpu.make_async_copy(
            src.at[heads], dst.at[core, :, here], own_sem.at[2 + kind]
        )
        copy.start()
        own.append(copy)
    wide = []
    for index, (dx, dc) in enumerate([(0, 0)] + peers):
        if index == 0:
            continue
        head = lax.rem(x + dx, NX) * 2 + lax.rem(core + dc, 2)
        for kind, (src, dst) in enumerate(((q, q_out), (g, g_out))):
            wide.append(
                send(
                    src.at[pl.ds(head * GROUP, GROUP)],
                    dst.at[core, :, here],
                    x_send.at[2 + kind, index],
                    x_recv.at[2 + kind, index],
                    peer(dx, dc),
                )
            )
    own[0].wait()
    own[1].wait()
    for copy in copies:
        copy.wait()
    for kind in range(2):
        for block in range(2):
            kv_rows[kind, block * ROWS : (block + 1) * ROWS, :] = (
                kv_in[kind, block].astype(F32).T.astype(BF16)
            )
    keep = pltpu.make_async_copy(kv_rows, kv_out.at[z], own_sem.at[4])
    keep.start()

    def ring(group, step):
        waits = []
        for way in range(2):
            if step == 1 and group == 0:
                src = kv_rows
                block = z
            else:
                block = lax.rem(z + NZ + (step - 1) * (1 if way else -1), NZ)
                src = kv_out.at[group * NZ + block]
            dst = kv_out.at[group * NZ + block]
            if step == 4:
                src, dst = src.at[way], dst.at[way]
            waits.append(
                send(
                    src, dst, z_send.at[group, way, step - 1], z_recv.at[group, way, step - 1],
                    down if way else up,
                )
            )
        return waits

    flying = [ring(0, 1), None]
    shift = send(kv_rows, kv_out.at[NZ + z], y_sem.at[0], y_sem.at[1], later)
    shift.wait_recv()
    flying[1] = ring(1, 1)
    sent = []
    for step in range(2, 5):
        for group in range(2):
            for copy in flying[group]:
                copy.wait_recv()
            sent.extend(flying[group])
            flying[group] = ring(group, step)
    for group in range(2):
        for copy in flying[group]:
            copy.wait_recv()
        sent.extend(flying[group])
    for copy in sent:
        copy.wait_send()
    shift.wait_send()
    keep.wait()
    own[2].wait()
    own[3].wait()
    for copy in wide:
        copy.wait()


def bring(q, k, v, g):
    return pl.pallas_call(
        bring_kernel,
        out_shape=(
            jax.ShapeDtypeStruct((2, GROUP, HD, ROWS), BF16),
            jax.ShapeDtypeStruct((2, GROUP, HD, ROWS), BF16),
            jax.ShapeDtypeStruct((2 * NZ, 2, 2 * ROWS, HD), BF16),
        ),
        in_specs=[ANY] * 4,
        out_specs=(ANY, ANY, ANY),
        scratch_shapes=[
            pltpu.VMEM((2, 2, HD, ROWS), BF16),
            pltpu.VMEM((2, 2 * ROWS, HD), BF16),
            pltpu.SemaphoreType.DMA((5,)),
            pltpu.SemaphoreType.DMA((4, 8)),
            pltpu.SemaphoreType.DMA((4, 8)),
            pltpu.SemaphoreType.DMA((2,)),
            pltpu.SemaphoreType.DMA((2, 2, 4)),
            pltpu.SemaphoreType.DMA((2, 2, 4)),
        ],
        compiler_params=pltpu.CompilerParams(
            collective_id=0, has_side_effects=True, vmem_limit_bytes=16 << 20
        ),
        name="bring",
    )(q, k, v, g)


def attend_kernel(
    order, docs, q, g, kv, attn, dq, dkv,
    q_cols, g_cols, q_rows, g_rows, scores, key_acc, value_acc, out_acc, rows_tmp, slot_list, base_list,
):
    outer = lax.axis_index("outer")
    chip = lax.div(lax.axis_index("inner"), 2)
    doc = docs[...]
    starts = [
        jnp.sum(jnp.where(doc < d, 1.0, 0.0)).astype(jnp.int32) for d in range(1, 4)
    ]

    def start_of(position):
        found = jnp.zeros_like(position)
        for start in starts:
            found = jnp.where(position >= start, jnp.maximum(found, start), found)
        return found

    key_acc[...] = jnp.zeros_like(key_acc)
    value_acc[...] = jnp.zeros_like(value_acc)

    low = lax.broadcasted_iota(jnp.int32, (HD, ROWS), 1) < SPAN

    @pl.loop(0, 8)
    def _(index):
        block = lax.div(index, 4)
        pair = lax.rem(index, 4)
        lanes = pl.ds(pl.multiple_of(pair * ROWS, ROWS), ROWS)
        for src, cols, rows in ((q, q_cols, q_rows), (g, g_cols, g_rows)):
            first = src[block, 2 * pair].astype(F32)
            second = src[block, 2 * pair + 1].astype(F32)
            halves = (
                jnp.where(low, first, pltpu.roll(second, SPAN, 1)),
                jnp.where(low, pltpu.roll(first, SPAN, 1), second),
            )
            for half in range(2):
                cols[2 * block + half, :, lanes] = halves[half].astype(BF16)
                rows[2 * block + half, lanes, :] = halves[half].T.astype(BF16)

    iota_keys = lax.broadcasted_iota(jnp.int32, (SPAN, 256), 0)
    iota_lanes = lax.rem(lax.broadcasted_iota(jnp.int32, (1, 256), 1), SPAN)

    @pl.loop(0, 4)
    def _(unit):
        query_span = order[outer * 32 + chip * 4 + unit]
        first_span = lax.div(start_of(query_span * SPAN), SPAN)

        def note(slot, count):
            stored = lax.rem(outer + 4 - lax.div(slot, 32), 4) * 32 + lax.rem(slot, 32)
            span = order[stored]
            slot_list[count] = slot
            base_list[count] = span * SPAN
            return count + jnp.where((span >= first_span) & (span <= query_span), 1, 0)

        count = lax.fori_loop(0, SLOTS, note, 0)
        for extra in range(4):
            slot_list[count + extra] = 0
            base_list[count + extra] = FAR
        chunks = lax.div(count + 3, 4)
        query_pos = query_span * SPAN + iota_lanes
        query_start = start_of(query_pos)

        def spans(chunk, kind):
            parts = []
            for part in range(4):
                slot = slot_list[chunk * 4 + part]
                parts.append(kv[lax.div(slot, 4), kind, lax.rem(slot, 4)])
            return jnp.concatenate(parts, axis=0)

        def score_step(chunk, tops):
            keys = spans(chunk, 0)
            new = []
            for side in range(2):
                lanes = pl.ds(side * 256, 256)
                tile = jnp.dot(keys, q_cols[unit, :, lanes], preferred_element_type=F32)
                top = tops[side]
                for part in range(4):
                    base = base_list[chunk * 4 + part]
                    allowed = (iota_keys <= query_pos - base) & (iota_keys >= query_start - base)
                    piece = jnp.where(allowed, tile[part * SPAN : (part + 1) * SPAN], NEG)
                    scores[chunk, pl.ds(part * SPAN, SPAN), lanes] = piece
                    top = jnp.maximum(top, jnp.max(piece.reshape(8, 8, 256), axis=0))
                new.append(top)
            return tuple(new)

        floor = jnp.full((8, 256), NEG, F32)
        tops = lax.fori_loop(0, chunks, score_step, (floor, floor))
        row_max = [jnp.max(top, axis=0, keepdims=True) for top in tops]
        out_acc[...] = jnp.zeros_like(out_acc)

        def value_step(chunk, sums):
            values_t = spans(chunk, 1).astype(F32).T.astype(BF16)
            new = []
            for side in range(2):
                lanes = pl.ds(side * 256, 256)
                probs = jnp.exp2((scores[chunk, :, lanes] - row_max[side]) * (SCALE * LOG2E))
                scores[chunk, :, lanes] = probs
                new.append(sums[side] + jnp.sum(probs.reshape(32, 8, 256), axis=0))
                out_acc[:, lanes] += jnp.dot(
                    values_t, probs.astype(BF16), preferred_element_type=F32
                )
            return tuple(new)

        nothing = jnp.zeros((8, 256), F32)
        sums = lax.fori_loop(0, chunks, value_step, (nothing, nothing))
        inverse = []
        row_dot = []
        half_rows = pl.ds(pl.multiple_of(lax.rem(unit, 2) * LANES, LANES), LANES)
        block = lax.div(unit, 2)
        for side in range(2):
            lanes = pl.ds(side * 256, 256)
            row_sum = jnp.sum(sums[side], axis=0, keepdims=True)
            inverse.append(1.0 / row_sum)
            out = (out_acc[:, lanes] / row_sum).astype(BF16).astype(F32)
            row_dot.append(
                jnp.sum(out * g_cols[unit, :, lanes].astype(F32), axis=0, keepdims=True)
            )
            out_t = out.T
            for part in range(4):
                rows_tmp[pl.ds(side * 4 + part, SPAN, stride=GROUP), :] = out_t[
                    part * SPAN : (part + 1) * SPAN
                ]
        attn[block, half_rows, :] = rows_tmp[...].astype(BF16)
        out_acc[...] = jnp.zeros_like(out_acc)

        def grad_step(chunk, _):
            keys = spans(chunk, 0)
            values = spans(chunk, 1)
            keys_t = keys.astype(F32).T.astype(BF16)
            key_part = None
            value_part = None
            for side in range(2):
                lanes = pl.ds(side * 256, 256)
                probs = scores[chunk, :, lanes] * inverse[side]
                prob_grads = jnp.dot(values, g_cols[unit, :, lanes], preferred_element_type=F32)
                score_grads = (probs * (prob_grads - row_dot[side])).astype(BF16)
                out_acc[:, lanes] += jnp.dot(keys_t, score_grads, preferred_element_type=F32)
                to_values = jnp.dot(
                    probs.astype(BF16), g_rows[unit, lanes, :], preferred_element_type=F32
                )
                to_keys = jnp.dot(score_grads, q_rows[unit, lanes, :], preferred_element_type=F32)
                value_part = to_values if side == 0 else value_part + to_values
                key_part = to_keys if side == 0 else key_part + to_keys
            for part in range(4):
                slot = slot_list[chunk * 4 + part]
                rows = slice(part * SPAN, (part + 1) * SPAN)
                key_acc[slot] += key_part[rows]
                value_acc[slot] += value_part[rows]
            return 0

        lax.fori_loop(0, chunks, grad_step, 0)
        for side in range(2):
            grad_t = (out_acc[:, pl.ds(side * 256, 256)] * SCALE).T
            for part in range(4):
                rows_tmp[pl.ds(side * 4 + part, SPAN, stride=GROUP), :] = grad_t[
                    part * SPAN : (part + 1) * SPAN
                ]
        dq[block, half_rows, :] = rows_tmp[...]

    @pl.loop(0, 2 * NZ)
    def _(index):
        for part in range(4):
            dkv[index, 0, part] = (key_acc[index * 4 + part] * SCALE).astype(BF16)
            dkv[index, 1, part] = value_acc[index * 4 + part].astype(BF16)


def attend(order, docs, q, g, kv):
    return pl.pallas_call(
        attend_kernel,
        out_shape=(
            jax.ShapeDtypeStruct((2, ROWS * GROUP, HD), BF16),
            jax.ShapeDtypeStruct((2, ROWS * GROUP, HD), F32),
            jax.ShapeDtypeStruct((2 * NZ, 2, 4, SPAN, HD), BF16),
        ),
        in_specs=[SMEM, VMEM, VMEM, VMEM, VMEM],
        out_specs=(VMEM, VMEM, VMEM),
        scratch_shapes=[
            pltpu.VMEM((4, HD, LANES), BF16),
            pltpu.VMEM((4, HD, LANES), BF16),
            pltpu.VMEM((4, LANES, HD), BF16),
            pltpu.VMEM((4, LANES, HD), BF16),
            pltpu.VMEM((SLOTS // 4, 4 * SPAN, LANES), F32),
            pltpu.VMEM((SLOTS, SPAN, HD), F32),
            pltpu.VMEM((SLOTS, SPAN, HD), F32),
            pltpu.VMEM((HD, LANES), F32),
            pltpu.VMEM((LANES, HD), F32),
            pltpu.SMEM((SLOTS + 8,), jnp.int32),
            pltpu.SMEM((SLOTS + 8,), jnp.int32),
        ],
        compiler_params=pltpu.CompilerParams(vmem_limit_bytes=48 << 20),
        cost_estimate=pl.CostEstimate(
            flops=6 * 2 * 2048 * 2048 * HD, bytes_accessed=12 << 20, transcendentals=2048 * 2048
        ),
        name="attend",
    )(order, docs, q, g, kv)


def return_kernel(
    attn, dq, dkv, attn_out, dq_out, dkv_out,
    landed, summed, from_later, final, pair_send, pair_recv, own_sem, y_sem, z_send, z_recv,
):
    x, y, z, core = place()
    sibling = where_is(x, y, z, 1 - core)
    up = where_is(x, y, lax.rem(z + 1, NZ), core)
    down = where_is(x, y, lax.rem(z + NZ - 1, NZ), core)
    later = where_is(x, lax.rem(y + 1, NY), z, core)
    earlier = where_is(x, lax.rem(y + NY - 1, NY), z, core)
    greet([sibling, up, down, later, earlier])

    def ring(group, step):
        sends = []
        for way in range(2):
            if step == 1:
                block = lax.rem(z + 4, NZ)
                src = dkv.at[group * NZ + block, way]
                dst = landed.at[group, way, 0, way]
            else:
                src = landed.at[group, way, step - 2]
                dst = landed.at[group, way, step - 1]
            sends.append(
                send(
                    src, dst, z_send.at[group, way, step - 1], z_recv.at[group, way, step - 1],
                    down if way else up,
                )
            )
        return sends

    def add(group, step):
        for way in range(2):
            block = lax.rem(z + NZ + (4 - step) * (-1 if way else 1), NZ)
            for kind in range(2):
                term = dkv[group * NZ + block, kind]
                if step > 1 or kind == way:
                    term = (
                        landed[group, way, step - 1, kind].astype(F32) + term.astype(F32)
                    ).astype(BF16)
                landed[group, way, step - 1, kind] = term

    flying = [None, None]
    flying[1] = ring(1, 1)
    flying[0] = ring(0, 1)
    swaps = []
    own = []
    for kind, (src, dst) in enumerate(((attn, attn_out), (dq, dq_out))):
        swaps.append(
            send(src.at[1 - core], dst.at[core], pair_send.at[kind], pair_recv.at[kind], sibling)
        )
        copy = pltpu.make_async_copy(src.at[core], dst.at[core], own_sem.at[kind])
        copy.start()
        own.append(copy)
    sent = []
    for step in range(1, 4):
        for group in (1, 0):
            for copy in flying[group]:
                copy.wait_recv()
            sent.extend(flying[group])
            add(group, step)
            flying[group] = ring(group, step + 1)
    back = None
    for group in (1, 0):
        for copy in flying[group]:
            copy.wait_recv()
        sent.extend(flying[group])
        for kind in range(2):
            total = (
                landed[group, 0, 3, kind].astype(F32)
                + landed[group, 1, 3, kind].astype(F32)
                + dkv[group * NZ + z, kind].astype(F32)
            )
            if group == 1:
                summed[kind] = total.astype(BF16)
            else:
                final[kind] = total
        if group == 1:
            back = send(summed, from_later, y_sem.at[0], y_sem.at[1], earlier)
    back.wait_recv()
    for kind in range(2):
        final[kind] = final[kind] + from_later[kind].astype(F32)
    mine = pl.ds(pl.multiple_of(core * ROWS, ROWS), ROWS)
    other = pl.ds(pl.multiple_of((1 - core) * ROWS, ROWS), ROWS)
    for kind in range(2):
        swaps.append(
            send(
                final.at[kind, other], dkv_out.at[kind, core],
                pair_send.at[2 + kind], pair_recv.at[2 + kind], sibling,
            )
        )
        copy = pltpu.make_async_copy(
            final.at[kind, mine], dkv_out.at[kind, core], own_sem.at[2 + kind]
        )
        copy.start()
        own.append(copy)
    for copy in sent:
        copy.wait_send()
    back.wait_send()
    for copy in swaps:
        copy.wait()
    for copy in own:
        copy.wait()


def give_back(attn, dq, dkv):
    return pl.pallas_call(
        return_kernel,
        out_shape=(
            jax.ShapeDtypeStruct((2, ROWS * GROUP, HD), BF16),
            jax.ShapeDtypeStruct((2, ROWS * GROUP, HD), F32),
            jax.ShapeDtypeStruct((2, 2, ROWS, HD), F32),
        ),
        in_specs=[ANY, ANY, VMEM],
        out_specs=(ANY, ANY, ANY),
        scratch_shapes=[
            pltpu.VMEM((2, 2, 4, 2, 2 * ROWS, HD), BF16),
            pltpu.VMEM((2, 2 * ROWS, HD), BF16),
            pltpu.VMEM((2, 2 * ROWS, HD), BF16),
            pltpu.VMEM((2, 2 * ROWS, HD), F32),
            pltpu.SemaphoreType.DMA((4,)),
            pltpu.SemaphoreType.DMA((4,)),
            pltpu.SemaphoreType.DMA((4,)),
            pltpu.SemaphoreType.DMA((2,)),
            pltpu.SemaphoreType.DMA((2, 2, 4)),
            pltpu.SemaphoreType.DMA((2, 2, 4)),
        ],
        compiler_params=pltpu.CompilerParams(
            collective_id=1, has_side_effects=True, vmem_limit_bytes=24 << 20
        ),
        name="give_back",
    )(attn, dq, dkv)


def local(queries, keys, values, grad_out, span_order, doc_ids):
    turned = [jnp.transpose(a, (1, 2, 0)) for a in (queries, keys, values, grad_out)]
    q, g, kv = bring(*turned)
    kv = kv.reshape(2 * NZ, 2, 4, SPAN, HD)
    attn, dq, dkv = attend(span_order, doc_ids.reshape(64, 128), q, g, kv)
    attn, dq, dkv = give_back(attn, dq, dkv.reshape(2 * NZ, 2, 2 * ROWS, HD))

    def join(halves):
        return (
            halves.reshape(2, ROWS, GROUP, HD)
            .transpose(1, 0, 2, 3)
            .reshape(ROWS, 2 * GROUP, HD)
        )

    grads = dkv.transpose(0, 2, 1, 3)
    return (join(attn), join(dq), grads[0], grads[1])


def solution(mesh):
    entry = P(("outer", "inner"), None, "head")
    leave = P(("outer", "inner"), "head", None)
    return jax.shard_map(
        local,
        mesh=mesh,
        in_specs=(entry, entry, entry, entry, P(), P()),
        out_specs=(leave, leave, leave, leave),
        check_vma=False,
    )
```

time: 499 us -> 113 us (0.23)
  the two profiles are of different devices: /device:TPU:26 before, /device:TPU:1 now
where the time goes in v1:
time: 113 us
  Pallas kernels  102 us (90%)
  local copies, waits for them, and re-layouts  9.96 us (9%)
    pallas_call x1, Pallas kernels, bring(): pl.pallas_call(bring_kernel, out_shape=(jax.ShapeDtypeStruct((2, GROUP, H...  38.8 us
    pallas_call x1, Pallas kernels, attend(): pl.pallas_call(attend_kernel, out_shape=(jax.ShapeDtypeStruct((2, ROWS *...  34.3 us
    pallas_call x1, Pallas kernels, give_back(): pl.pallas_call(return_kernel, out_shape=(jax.ShapeDtypeStruct((2, ROWS *...  29.3 us
    unnamed x16, local copies, waits for them, and re-layouts  8.01 us

profile of v1, /device:TPU:1, one launch (start us, length us, event | category | flops | bytes accessed | tf_op | source)
XLA Modules:
  0.0 112.9 jit_solution(16787429060959401973)
XLA Ops:
  0.6 0.0 copy-start
  0.6 1.0 copy-done
  1.7 0.0 copy-start.1
  1.7 1.0 copy-done.1
  2.7 0.0 copy-start.2
  2.7 0.8 copy-done.2
  3.6 0.0 copy-start.3
  3.6 0.8 copy-done.3
  4.4 38.8 %bring.1 = (bf16[2,8,128,128]{3,2,1,0:T(8,128)(2,1)S(1)}, bf16[2,8,128,128]{3,2,1,0:T(8,128)(2,1)S(1)}, bf16[16,2,256,128]{3,2,1,0:T(8,128)(2,1)S(1)}) custom-call(bf16[64,32,128]{2,1,0:T(8,128)(2,1)S(1)} %bitcast.27, bf16[8,32,128]{2,1,0:T(8,128)(2,1)S(1)} %bitcast.30, bf16[8,32,128]{2,1,0:T(8,128)(2,1)S(1)} %bitcast.31, bf16[64,32,128]{2,1,0:T(8,128)(2,1)S(1)} %bitcast.28), custom_call_target="tpu_custom_call" | custom-call | tf_op jit(solution)/shard_map/bring/pallas_call | solution.py:177
  43.2 0.0 copy-start.4
  43.2 1.3 %copy-done.4 = bf16[16,2,256,128]{3,2,1,0:T(8,128)(2,1)} copy-done((bf16[16,2,256,128]{3,2,1,0:T(8,128)(2,1)}, bf16[16,2,256,128]{3,2,1,0:T(8,128)(2,1)S(1)}, u32[]{:S(2)}) %copy-start.4) | copy-done | bytes 2097176
  44.5 0.0 copy-start.5
  44.5 0.8 copy-done.5
  45.3 0.0 copy-start.6
  45.3 0.7 copy-done.6
  45.9 34.3 %attend.1 = (bf16[2,1024,128]{2,1,0:T(8,128)(2,1)S(1)}, f32[2,1024,128]{2,1,0:T(8,128)S(1)}, bf16[16,2,4,64,128]{4,3,2,1,0:T(8,128)(2,1)S(1)}) custom-call(s32[128]{0:T(128)S(1)} %copy-done.6, s32[64,128]{1,0:T(8,128)S(1)} %bitcast.33, bf16[2,8,128,128]{3,2,1,0:T(8,128)(2,1)S(1)} %get-tuple-element.13.q, bf16[2,8,128,128]{3,2,1,0:T(8,128)(2,1)S(1)} %get-tuple-element.14.g, ...), custom_call_target="tpu_custom_call" | custom-call | flops 6442450944 | bytes 12582912 | tf_op jit(solution)/shard_map/attend/pallas_call | solution.py:369
  80.2 29.3 %give_back.1 = (bf16[2,1024,128]{2,1,0:T(8,128)(2,1)S(1)}, f32[2,1024,128]{2,1,0:T(8,128)S(1)}, f32[2,2,128,128]{3,2,1,0:T(8,128)S(1)}) custom-call(bf16[2,1024,128]{2,1,0:T(8,128)(2,1)S(1)} %get-tuple-element.16.attn, f32[2,1024,128]{2,1,0:T(8,128)S(1)} %get-tuple-element.17.dq, bf16[16,2,256,128]{3,2,1,0:T(8,128)(2,1)S(1)} %bitcast.26), custom_call_target="tpu_custom_call" | custom-call | tf_op jit(solution)/shard_map/give_back/pallas_call | solution.py:504
  109.5 0.9 copy_bitcast_fusion.1
  110.4 0.8 copy.13
  111.1 0.8 copy.12
  111.9 1.1 copy_bitcast_fusion
  (1 shorter events, 0.0 us)
Async XLA Ops:
  0.6 1.0 copy-start
  1.7 1.0 copy-start.1
  2.7 0.8 copy-start.2
  3.6 0.8 copy-start.3
  43.2 1.3 %copy-start.4 = (bf16[16,2,256,128]{3,2,1,0:T(8,128)(2,1)}, bf16[16,2,256,128]{3,2,1,0:T(8,128)(2,1)S(1)}, u32[]{:S(2)}) copy-start(bf16[16,2,256,128]{3,2,1,0:T(8,128)(2,1)S(1)} %get-tuple-element.15) | copy-start | bytes 6291460
  44.5 0.8 copy-start.5
  45.3 0.7 copy-start.6

commit v2 on v1

v2 whole, which is shorter than its diff:
```python
import functools
import math

import jax
import jax.numpy as jnp
from jax import lax
from jax.experimental import pallas as pl
from jax.experimental.pallas import tpu as pltpu
from jax.sharding import PartitionSpec as P

MESH = pl.DeviceIdType.MESH
HBM = pl.BlockSpec(memory_space=pltpu.HBM)
NEG = -1e30
FAR = 1 << 24
NX = 4
NY = 4
NZ = 8
HD = 128
ROWS = 128
SPAN = 64
GROUP = 8
SLOTS = 64
LANES = GROUP * SPAN
SCALE = 1.0 / math.sqrt(HD)
LOG2E = math.log2(math.e)
ITEM = 4
BF16 = jnp.bfloat16
F32 = jnp.float32


def place():
    inner = lax.axis_index("inner")
    return (
        lax.axis_index("head"),
        lax.axis_index("outer"),
        lax.div(inner, 2),
        lax.rem(inner, 2),
    )


def where_is(x, y, z, core):
    return {"head": x, "outer": y, "inner": z * 2 + core}


def greet(partners):
    barrier = pltpu.get_barrier_semaphore()
    for partner in partners:
        pl.semaphore_signal(barrier, inc=1, device_id=partner, device_id_type=MESH)
    pl.semaphore_wait(barrier, len(partners))


def send(src, dst, send_sem, recv_sem, partner):
    copy = pltpu.make_async_remote_copy(
        src_ref=src,
        dst_ref=dst,
        send_sem=send_sem,
        recv_sem=recv_sem,
        device_id=partner,
        device_id_type=MESH,
    )
    copy.start()
    return copy


def bring_kernel(
    q, k, v, g, q_cols_out, g_cols_out, q_rows_out, g_rows_out, kv_out,
    q_cols, g_cols, q_rows, g_rows, out_sem, q_in, g_in, kv_in, ring_kv, own_sem, keep_sem, x_send, x_recv, y_send, y_recv, z_send, z_recv,
):
    x, y, z, core = place()
    peers = [(dx, dc) for dx in range(NX) for dc in range(2) if (dx, dc) != (0, 0)]

    def peer(dx, dc):
        return where_is(lax.rem(x + dx, NX), y, z, lax.rem(core + dc, 2))

    up = where_is(x, y, lax.rem(z + 1, NZ), core)
    down = where_is(x, y, lax.rem(z + NZ - 1, NZ), core)
    later = where_is(x, lax.rem(y + 1, NY), z, core)
    earlier = where_is(x, lax.rem(y + NY - 1, NY), z, core)
    greet([peer(*p) for p in peers] + [up, down, later, earlier])

    here = pl.ds(pl.multiple_of(x * 32, 32), 32)
    copies = []
    own = []
    for index, (dx, dc) in enumerate([(0, 0)] + peers):
        head = lax.rem(x + dx, NX) * 2 + lax.rem(core + dc, 2)
        for kind, src in enumerate((k, v)):
            dst = kv_in.at[kind, core, here]
            if index == 0:
                copy = pltpu.make_async_copy(src.at[head], dst, own_sem.at[kind])
                copy.start()
                own.append(copy)
            else:
                copies.append(
                    send(src.at[head], dst, x_send.at[kind, index], x_recv.at[kind, index], peer(dx, dc))
                )
    own[0].wait()
    own[1].wait()
    for copy in copies:
        copy.wait()
    for kind in range(2):
        for block in range(2):
            ring_kv[z, kind, block * ROWS : (block + 1) * ROWS, :] = (
                kv_in[kind, block].astype(F32).T.astype(BF16)
            )
    keeps = []
    sent = []
    ways = (up, down)

    def block_at(group, way, step):
        return group * NZ + lax.rem(z + NZ + step * (1 if way else -1), NZ)

    def keep(block, index):
        copy = pltpu.make_async_copy(ring_kv.at[block], kv_out.at[block], keep_sem.at[index])
        copy.start()
        keeps.append(copy)

    def hop(group, way, step, kind):
        block = block_at(group, way, step - 1)
        copy = send(
            ring_kv.at[block, kind], ring_kv.at[block, kind],
            z_send.at[group, way, step - 1, kind], z_recv.at[group, way, step - 1, kind],
            ways[way],
        )
        sent.append(copy)
        return copy

    def shift(way, step, kind):
        block = block_at(0, way, step)
        copy = send(
            ring_kv.at[block, kind], ring_kv.at[NZ + block, kind],
            y_send.at[way, step // 2, kind], y_recv.at[way, step // 2, kind], later,
        )
        sent.append(copy)
        return copy

    def settle(kind):
        src, cols, rows = ((q_in, q_cols, q_rows), (g_in, g_cols, g_rows))[kind]
        own[2 + kind].wait()
        for copy in wide[kind]:
            copy.wait()
        low = lax.broadcasted_iota(jnp.int32, (HD, ROWS), 1) < SPAN

        @pl.loop(0, 8)
        def _(index):
            block = lax.div(index, 4)
            pair = lax.rem(index, 4)
            lanes = pl.ds(pl.multiple_of(pair * ROWS, ROWS), ROWS)
            first = src[block, 2 * pair].astype(F32)
            second = src[block, 2 * pair + 1].astype(F32)
            halves = (
                jnp.where(low, first, pltpu.roll(second, SPAN, 1)),
                jnp.where(low, pltpu.roll(first, SPAN, 1), second),
            )
            for half in range(2):
                cols[2 * block + half, :, lanes] = halves[half].astype(BF16)
                rows[2 * block + half, lanes, :] = halves[half].T.astype(BF16)

        outs = ((q_cols_out, q_rows_out), (g_cols_out, g_rows_out))[kind]
        for index, (src, dst) in enumerate(zip((cols, rows), outs)):
            copy = pltpu.make_async_copy(src, dst, out_sem.at[kind, index])
            copy.start()
            own.append(copy)

    near = {}
    self_shift = {}
    for kind in range(2):
        for way in range(2):
            near[way, 1, kind] = hop(0, way, 1, kind)
        self_shift[kind] = shift(0, 0, kind)
    keep(z, 0)
    heads = pl.ds((x * 2 + core) * GROUP, GROUP)
    for kind, (src, dst) in enumerate(((q, q_in), (g, g_in))):
        copy = pltpu.make_async_copy(
            src.at[heads], dst.at[core, :, here], own_sem.at[2 + kind]
        )
        copy.start()
        own.append(copy)
    wide = ([], [])
    for kind, (src, dst) in enumerate(((q, q_in), (g, g_in))):
        for index, (dx, dc) in enumerate(peers):
            head = lax.rem(x + dx, NX) * 2 + lax.rem(core + dc, 2)
            wide[kind].append(
                send(
                    src.at[pl.ds(head * GROUP, GROUP)],
                    dst.at[core, :, here],
                    x_send.at[2 + kind, index],
                    x_recv.at[2 + kind, index],
                    peer(dx, dc),
                )
            )
    far_shift = {}
    for step in range(1, 4):
        for kind in range(2):
            for way in range(2):
                near[way, step, kind].wait_recv()
                if step < 3 or kind == way:
                    near[way, step + 1, kind] = hop(0, way, step + 1, kind)
                if step == 2:
                    far_shift[way, kind] = shift(way, 2, kind)
        for way in range(2):
            keep(block_at(0, way, step), 1 + 2 * step + way)
    hops = {}
    for kind in range(2):
        self_shift[kind].wait_recv()
        for way in range(2):
            hops[way, 1, kind] = hop(1, way, 1, kind)
    keep(NZ + z, 1)
    last_shift = []
    for way in range(2):
        near[way, 4, way].wait_recv()
        last_shift.append(shift(way, 4, way))
    keep(block_at(0, 0, 4), 2)
    for kind in range(2):
        for way in range(2):
            far_shift[way, kind].wait_recv()
            hops[way, 3, kind] = hop(1, way, 3, kind)
    for way in range(2):
        keep(block_at(1, way, 2), 9 + way)
    settle(0)
    for step in (1, 3):
        for way in range(2):
            for kind in range(2):
                hops[way, step, kind].wait_recv()
            keep(block_at(1, way, step), 10 + step + way)
        if step == 1:
            for way in range(2):
                last_shift[way].wait_recv()
            keep(block_at(1, 0, 4), 15)
            settle(1)
    for copy in sent:
        copy.wait_send()
    for copy in keeps:
        copy.wait()
    for copy in own[4:]:
        copy.wait()


def bring(q, k, v, g):
    return pl.pallas_call(
        bring_kernel,
        out_shape=(
            jax.ShapeDtypeStruct((4, HD, LANES), BF16),
            jax.ShapeDtypeStruct((4, HD, LANES), BF16),
            jax.ShapeDtypeStruct((4, LANES, HD), BF16),
            jax.ShapeDtypeStruct((4, LANES, HD), BF16),
            jax.ShapeDtypeStruct((2 * NZ, 2, 2 * ROWS, HD), BF16),
        ),
        in_specs=[HBM] * 4,
        out_specs=(HBM,) * 5,
        scratch_shapes=[
            pltpu.VMEM((4, HD, LANES), BF16),
            pltpu.VMEM((4, HD, LANES), BF16),
            pltpu.VMEM((4, LANES, HD), BF16),
            pltpu.VMEM((4, LANES, HD), BF16),
            pltpu.SemaphoreType.DMA((2, 2)),
            pltpu.VMEM((2, GROUP, HD, ROWS), BF16),
            pltpu.VMEM((2, GROUP, HD, ROWS), BF16),
            pltpu.VMEM((2, 2, HD, ROWS), BF16),
            pltpu.VMEM((2 * NZ, 2, 2 * ROWS, HD), BF16),
            pltpu.SemaphoreType.DMA((4,)),
            pltpu.SemaphoreType.DMA((16,)),
            pltpu.SemaphoreType.DMA((4, 8)),
            pltpu.SemaphoreType.DMA((4, 8)),
            pltpu.SemaphoreType.DMA((2, 3, 2)),
            pltpu.SemaphoreType.DMA((2, 3, 2)),
            pltpu.SemaphoreType.DMA((2, 2, 4, 2)),
            pltpu.SemaphoreType.DMA((2, 2, 4, 2)),
        ],
        compiler_params=pltpu.CompilerParams(
            collective_id=0, has_side_effects=True, vmem_limit_bytes=60 << 20
        ),
        name="bring",
    )(q, k, v, g)


def attend_kernel(
    order_in, docs_in, q_cols_in, g_cols_in, q_rows_in, g_rows_in, kv_in, attn_out, dq_out, dkv,
    order, docs, q_cols, g_cols, q_rows, g_rows, attn, dq, kv, scores, key_acc, value_acc, out_acc, tops, sums, shift, dots,
    pos_rows, start_rows, item_list, span_list, in_sem, out_sem,
):
    outer = lax.axis_index("outer")
    chip = lax.div(lax.axis_index("inner"), 2)
    loads = [
        pltpu.make_async_copy(order_in, order, in_sem.at[0]),
        pltpu.make_async_copy(docs_in, docs, in_sem.at[1]),
        pltpu.make_async_copy(q_cols_in, q_cols, in_sem.at[2]),
        pltpu.make_async_copy(kv_in.at[:, 0], kv.at[:, 0], in_sem.at[3]),
        pltpu.make_async_copy(kv_in.at[:, 1], kv.at[:, 1], in_sem.at[4]),
        pltpu.make_async_copy(g_cols_in, g_cols, in_sem.at[5]),
        pltpu.make_async_copy(q_rows_in, q_rows, in_sem.at[6]),
        pltpu.make_async_copy(g_rows_in, g_rows, in_sem.at[7]),
    ]
    for load in loads:
        load.start()
    key_acc[...] = jnp.zeros_like(key_acc)
    value_acc[...] = jnp.zeros_like(value_acc)
    out_acc[...] = jnp.zeros_like(out_acc)
    dq[...] = jnp.zeros_like(dq)
    tops[...] = jnp.full_like(tops, NEG)
    sums[...] = jnp.zeros_like(sums)
    loads[0].wait()
    loads[1].wait()
    doc = docs[...]
    starts = [
        jnp.sum(jnp.where(doc < d, 1.0, 0.0)).astype(jnp.int32) for d in range(1, 4)
    ]

    def start_of(position):
        found = jnp.zeros_like(position)
        for start in starts:
            found = jnp.where(position >= start, jnp.maximum(found, start), found)
        return found

    iota_lanes = lax.rem(lax.broadcasted_iota(jnp.int32, (8, ROWS), 1), SPAN)
    lows = []
    highs = []
    for unit in range(4):
        query_span = order[outer * 32 + chip * 4 + unit]
        lows.append(lax.div(start_of(query_span * SPAN), SPAN))
        highs.append(query_span)
        query_pos = query_span * SPAN + iota_lanes
        pos_rows[unit] = query_pos
        start_rows[unit] = start_of(query_pos)

    counts = tuple(jnp.int32(unit * 128) for unit in range(4))
    for group in range(2):
        stored = lax.rem(outer + 4 - group, 4) * 32

        def note(step, counts):
            for part in range(8):
                slot = step * 8 + part
                span = order[stored + slot]
                entry = span * SPAN + (group * 32 + slot)
                new = []
                for unit in range(4):
                    span_list[counts[unit]] = entry
                    allowed = (span >= lows[unit]) & (span <= highs[unit])
                    new.append(counts[unit] + jnp.where(allowed, 1, 0))
                counts = tuple(new)
            return counts

        counts = lax.fori_loop(0, 4, note, counts)
    items = jnp.int32(0)
    for unit in range(4):
        for extra in range(ITEM):
            span_list[counts[unit] + extra] = FAR
        for chunk in range(SLOTS // ITEM):
            item_list[items + chunk] = unit * 128 + chunk * ITEM
        items = items + lax.div(counts[unit] - unit * 128 + ITEM - 1, ITEM)
    blank = 3 * 128 + 72
    for extra in range(ITEM):
        span_list[blank + extra] = FAR
    item_list[items] = blank
    steps = lax.div(items + 1, 2)

    iota_keys = (
        lax.broadcasted_iota(jnp.int32, (8, 8, ROWS), 0) * 8
        + lax.broadcasted_iota(jnp.int32, (8, 8, ROWS), 1)
    )

    def entries(item):
        first = item_list[item]
        found = [span_list[first + part] for part in range(ITEM)]
        slots = [lax.rem(entry, SLOTS) for entry in found]
        return lax.div(first, 128), slots, [a - b for a, b in zip(found, slots)]

    def spans(slots, kind):
        parts = []
        for slot in slots:
            parts.append(kv[lax.div(slot, 4), kind, lax.rem(slot, 4)])
        return jnp.concatenate(parts, axis=0)

    sides = [pl.ds(side * 256, 256) for side in range(2)]
    loads[2].wait()
    loads[3].wait()

    @functools.partial(lax.fori_loop, 0, steps, init_val=0)
    def _(step, _):
        results = []
        for item in (2 * step, 2 * step + 1):
            unit, slots, bases = entries(item)
            keys = spans(slots, 0)
            biases = []
            for base in bases:
                allowed = (iota_keys <= (pos_rows[unit] - base)[None]) & (
                    iota_keys >= (start_rows[unit] - base)[None]
                )
                biases.append(jnp.where(allowed, 0.0, NEG).reshape(SPAN, ROWS))
            bias = jnp.concatenate(biases, axis=0)
            bias = jnp.concatenate([bias, bias], axis=1)
            for lanes in sides:
                tile = jnp.dot(keys, q_cols[unit, :, lanes], preferred_element_type=F32)
                tile = tile * (SCALE * LOG2E) + bias
                scores[item, :, lanes] = tile
                results.append((unit, lanes, jnp.max(tile.reshape(32, 8, 256), axis=0)))
        for unit, lanes, top in results:
            tops[unit, :, lanes] = jnp.maximum(tops[unit, :, lanes], top)
        return 0

    for unit in range(4):
        shift[unit] = jnp.broadcast_to(jnp.max(tops[unit], axis=0, keepdims=True), (8, LANES))
    loads[4].wait()

    @functools.partial(lax.fori_loop, 0, steps, init_val=0)
    def _(step, _):
        results = []
        for item in (2 * step, 2 * step + 1):
            unit, slots, _ = entries(item)
            values_t = spans(slots, 1).T
            for lanes in sides:
                logits = scores[item, :, lanes].reshape(32, 8, 256)
                probs = jnp.exp2(logits - shift[unit, :, lanes][None])
                part = jnp.dot(
                    values_t, probs.reshape(256, 256).astype(BF16), preferred_element_type=F32
                )
                results.append((unit, lanes, jnp.sum(probs, axis=0), part))
        for unit, lanes, total, part in results:
            sums[unit, :, lanes] += total
            out_acc[unit, :, lanes] += part
        return 0

    for load in loads[5:]:
        load.wait()
    for unit in range(4):
        row_sum = jnp.sum(sums[unit], axis=0, keepdims=True)
        out = (out_acc[unit] * (1.0 / row_sum)).astype(BF16)
        attn[unit] = out
        row_dot = jnp.sum(
            out.astype(F32) * g_cols[unit].astype(F32), axis=0, keepdims=True
        )
        dots[unit] = jnp.broadcast_to(row_dot, (8, LANES))
        shift[unit] = shift[unit] + jnp.log(row_sum) * LOG2E
    attn_store = pltpu.make_async_copy(attn, attn_out, out_sem.at[2 * NZ])
    attn_store.start()

    @functools.partial(lax.fori_loop, 0, steps, init_val=0)
    def _(step, _):
        results = []
        for item in (2 * step, 2 * step + 1):
            unit, slots, _ = entries(item)
            keys = spans(slots, 0)
            values = spans(slots, 1)
            keys_t = keys.T
            probs_b = []
            score_grads = []
            for lanes in sides:
                logits = scores[item, :, lanes].reshape(32, 8, 256)
                probs = jnp.exp2(logits - shift[unit, :, lanes][None])
                grads = jnp.dot(values, g_cols[unit, :, lanes], preferred_element_type=F32)
                grads = probs * (grads.reshape(32, 8, 256) - dots[unit, :, lanes][None])
                probs_b.append(probs.reshape(256, 256).astype(BF16))
                score_grads.append(grads.reshape(256, 256).astype(BF16))
            probs_b = jnp.concatenate(probs_b, axis=1)
            score_grads = jnp.concatenate(score_grads, axis=1)
            to_values = jnp.dot(probs_b, g_rows[unit], preferred_element_type=F32)
            to_keys = jnp.dot(score_grads, q_rows[unit], preferred_element_type=F32)
            to_query = jnp.dot(keys_t, score_grads, preferred_element_type=F32)
            results.append((slots, unit, to_values, to_keys, to_query))
        for slots, unit, to_values, to_keys, to_query in results:
            dq[unit] += to_query
            for part, slot in enumerate(slots):
                rows = slice(part * SPAN, (part + 1) * SPAN)
                key_acc[slot] += to_keys[rows]
                value_acc[slot] += to_values[rows]
        return 0

    dq_store = pltpu.make_async_copy(dq, dq_out, out_sem.at[2 * NZ + 1])
    dq_store.start()
    stores = [attn_store, dq_store]
    for index in range(2 * NZ):
        for part in range(4):
            kv[index, 0, part] = (key_acc[index * 4 + part] * SCALE).astype(BF16)
            kv[index, 1, part] = value_acc[index * 4 + part].astype(BF16)
        store = pltpu.make_async_copy(kv.at[index], dkv.at[index], out_sem.at[index])
        store.start()
        stores.append(store)
    for store in stores:
        store.wait()


def attend(order, docs, q_cols, g_cols, q_rows, g_rows, kv):
    return pl.pallas_call(
        attend_kernel,
        out_shape=(
            jax.ShapeDtypeStruct((4, HD, LANES), BF16),
            jax.ShapeDtypeStruct((4, HD, LANES), F32),
            jax.ShapeDtypeStruct((2 * NZ, 2, 4, SPAN, HD), BF16),
        ),
        in_specs=[HBM] * 7,
        out_specs=(HBM,) * 3,
        scratch_shapes=[
            pltpu.SMEM((2 * SLOTS,), jnp.int32),
            pltpu.VMEM((SLOTS, ROWS), jnp.int32),
            pltpu.VMEM((4, HD, LANES), BF16),
            pltpu.VMEM((4, HD, LANES), BF16),
            pltpu.VMEM((4, LANES, HD), BF16),
            pltpu.VMEM((4, LANES, HD), BF16),
            pltpu.VMEM((4, HD, LANES), BF16),
            pltpu.VMEM((4, HD, LANES), F32),
            pltpu.VMEM((2 * NZ, 2, 4, SPAN, HD), BF16),
            pltpu.VMEM((4 * SLOTS // ITEM, ITEM * SPAN, LANES), F32),
            pltpu.VMEM((SLOTS, SPAN, HD), F32),
            pltpu.VMEM((SLOTS, SPAN, HD), F32),
            pltpu.VMEM((4, HD, LANES), F32),
            pltpu.VMEM((4, 8, LANES), F32),
            pltpu.VMEM((4, 8, LANES), F32),
            pltpu.VMEM((4, 8, LANES), F32),
            pltpu.VMEM((4, 8, LANES), F32),
            pltpu.VMEM((4, 8, ROWS), jnp.int32),
            pltpu.VMEM((4, 8, ROWS), jnp.int32),
            pltpu.SMEM((80,), jnp.int32),
            pltpu.SMEM((512,), jnp.int32),
            pltpu.SemaphoreType.DMA((8,)),
            pltpu.SemaphoreType.DMA((2 * NZ + 2,)),
        ],
        compiler_params=pltpu.CompilerParams(vmem_limit_bytes=60 << 20),
        cost_estimate=pl.CostEstimate(
            flops=6 * 2 * 2048 * 2048 * HD, bytes_accessed=12 << 20, transcendentals=2048 * 2048
        ),
        name="attend",
    )(order, docs, q_cols, g_cols, q_rows, g_rows, kv)


def return_kernel(
    attn_in, dq_in, dkv, attn_out, dq_out, dkv_out,
    attn, dq, terms, attn_rows, dq_rows, rows_tmp, landed, final, pair_send, pair_recv, own_sem, l_send, l_recv,
):
    x, y, z, core = place()
    sibling = where_is(x, y, z, 1 - core)
    up = where_is(x, y, lax.rem(z + 1, NZ), core)
    down = where_is(x, y, lax.rem(z + NZ - 1, NZ), core)
    later = where_is(x, lax.rem(y + 1, NY), z, core)
    earlier = where_is(x, lax.rem(y + NY - 1, NY), z, core)
    loads = [
        pltpu.make_async_copy(attn_in, attn, own_sem.at[5]),
        pltpu.make_async_copy(dq_in, dq, own_sem.at[6]),
        pltpu.make_async_copy(dkv, terms, own_sem.at[4]),
    ]
    for load in loads:
        load.start()
    greet([sibling, up, down, later, earlier])

    ways = (up, down)
    sent = []

    def at(group, distance, way):
        return group * NZ + lax.rem(z + NZ + distance * (-1 if way else 1), NZ)

    def ship(src, index, partner):
        copy = send(src, landed.at[index], l_send.at[index], l_recv.at[index], partner)
        sent.append(copy)
        return copy

    def add(block, kind, *indices):
        total = terms[block, kind].astype(F32)
        for index in indices:
            total = total + landed[index].astype(F32)
        terms[block, kind] = total.astype(BF16)

    flying = {}
    for step, distance in ((0, 3), (1, 1)):
        for kind in range(2):
            for way in range(2):
                flying["z", step, way, kind] = ship(
                    dkv.at[at(1, distance, way), kind], step * 4 + way * 2 + kind, ways[way]
                )
        if step == 0:
            for kind in range(2):
                flying["y", 4, kind] = ship(dkv.at[at(1, 4, 0), kind], 8 + kind, earlier)
    swaps = []
    own = []

    def turn(block):
        for half in range(2):
            unit = 2 * block + half
            rows = pl.ds(half * LANES, LANES)
            for source, scale, target in ((attn, None, rows_tmp), (dq, SCALE, dq_rows.at[block, rows])):
                for pair in range(4):
                    tile = source[unit, :, pair * ROWS : (pair + 1) * ROWS].astype(F32)
                    tile = tile.T if scale is None else (tile * scale).T
                    for part in range(2):
                        target[pl.ds(2 * pair + part, SPAN, stride=GROUP), :] = tile[
                            part * SPAN : (part + 1) * SPAN
                        ]
                if scale is None:
                    attn_rows[block, rows, :] = rows_tmp[...].astype(BF16)

    def swap():
        turn(1 - core)
        for kind, (src, dst) in enumerate(((attn_rows, attn_out), (dq_rows, dq_out))):
            swaps.append(
                send(src.at[1 - core], dst.at[core], pair_send.at[kind], pair_recv.at[kind], sibling)
            )

    def stay():
        turn(core)
        for kind, (src, dst) in enumerate(((attn_rows, attn_out), (dq_rows, dq_out))):
            copy = pltpu.make_async_copy(src.at[core], dst.at[core], own_sem.at[kind])
            copy.start()
            own.append(copy)

    loads[2].wait()
    for kind in range(2):
        for way in range(2):
            flying["z", 0, way, kind].wait_recv()
            block = at(1, 2, way)
            add(block, kind, way * 2 + kind)
            flying["y", 2, way, kind] = ship(
                terms.at[block, kind], 10 + way * 2 + kind, earlier
            )
    for way in range(2):
        flying["y", 4, way].wait_recv()
        block = at(0, 4, 0)
        add(block, way, 8 + way)
        flying["s", 1, way, way] = ship(terms.at[block, way], 16 + way, ways[way])
    for way in range(2):
        kind = 1 - way
        flying["s", 2, way, kind] = ship(
            terms.at[at(0, 3, way), kind], 18 + way * 2 + kind, ways[way]
        )
    loads[0].wait()
    loads[1].wait()
    swap()
    for way in range(2):
        flying["s", 1, way, way].wait_recv()
        add(at(0, 3, way), way, 16 + way)
        flying["s", 2, way, way] = ship(
            terms.at[at(0, 3, way), way], 18 + way * 2 + way, ways[way]
        )
    for kind in range(2):
        for way in range(2):
            flying["z", 1, way, kind].wait_recv()
        add(NZ + z, kind, 4 + kind, 6 + kind)
        flying["y", 0, kind] = ship(terms.at[NZ + z, kind], 14 + kind, earlier)
    for step in (3, 4):
        for turn_of in range(2):
            for way in range(2):
                kind = turn_of if way else 1 - turn_of
                flying["s", step - 1, way, kind].wait_recv()
                indices = [18 + (step - 3) * 4 + way * 2 + kind]
                if step == 3:
                    flying["y", 2, way, kind].wait_recv()
                    indices.append(10 + way * 2 + kind)
                block = at(0, 5 - step, way)
                add(block, kind, *indices)
                flying["s", step, way, kind] = ship(
                    terms.at[block, kind], 18 + (step - 2) * 4 + way * 2 + kind, ways[way]
                )
        if step == 3:
            stay()
    for kind in range(2):
        flying["y", 0, kind].wait_recv()
        for way in range(2):
            flying["s", 4, way, kind].wait_recv()
        total = terms[z, kind].astype(F32)
        for index in (14 + kind, 26 + kind, 28 + kind):
            total = total + landed[index].astype(F32)
        final[kind] = total
    mine = pl.ds(pl.multiple_of(core * ROWS, ROWS), ROWS)
    other = pl.ds(pl.multiple_of((1 - core) * ROWS, ROWS), ROWS)
    for kind in range(2):
        swaps.append(
            send(
                final.at[kind, other], dkv_out.at[kind, core],
                pair_send.at[2 + kind], pair_recv.at[2 + kind], sibling,
            )
        )
        copy = pltpu.make_async_copy(
            final.at[kind, mine], dkv_out.at[kind, core], own_sem.at[2 + kind]
        )
        copy.start()
        own.append(copy)
    for copy in sent:
        copy.wait_send()
    for copy in swaps:
        copy.wait()
    for copy in own:
        copy.wait()


def give_back(attn, dq, dkv):
    return pl.pallas_call(
        return_kernel,
        out_shape=(
            jax.ShapeDtypeStruct((2, ROWS * GROUP, HD), BF16),
            jax.ShapeDtypeStruct((2, ROWS * GROUP, HD), F32),
            jax.ShapeDtypeStruct((2, 2, ROWS, HD), F32),
        ),
        in_specs=[HBM] * 3,
        out_specs=(HBM,) * 3,
        scratch_shapes=[
            pltpu.VMEM((4, HD, LANES), BF16),
            pltpu.VMEM((4, HD, LANES), F32),
            pltpu.VMEM((2 * NZ, 2, 2 * ROWS, HD), BF16),
            pltpu.VMEM((2, ROWS * GROUP, HD), BF16),
            pltpu.VMEM((2, ROWS * GROUP, HD), F32),
            pltpu.VMEM((LANES, HD), F32),
            pltpu.VMEM((30, 2 * ROWS, HD), BF16),
            pltpu.VMEM((2, 2 * ROWS, HD), F32),
            pltpu.SemaphoreType.DMA((4,)),
            pltpu.SemaphoreType.DMA((4,)),
            pltpu.SemaphoreType.DMA((7,)),
            pltpu.SemaphoreType.DMA((30,)),
            pltpu.SemaphoreType.DMA((30,)),
        ],
        compiler_params=pltpu.CompilerParams(
            collective_id=1, has_side_effects=True, vmem_limit_bytes=60 << 20
        ),
        name="give_back",
    )(attn, dq, dkv)


def finish_kernel(
    attn, dq, dkv, attn_out, dq_out, dk_out, dv_out, halves, joined, wide, wide_joined, parts, dk, dv, sem
):
    loads = [
        pltpu.make_async_copy(dkv, parts, sem.at[0]),
        pltpu.make_async_copy(attn, halves, sem.at[1]),
        pltpu.make_async_copy(dq, wide, sem.at[2]),
    ]
    for load in loads:
        load.start()
    stores = []
    loads[0].wait()
    for kind, (rows, dst) in enumerate(((dk, dk_out), (dv, dv_out))):
        for half in range(2):
            rows[pl.ds(half, ROWS, stride=2), :] = parts[kind, half]
        store = pltpu.make_async_copy(rows, dst, sem.at[4 + kind])
        store.start()
        stores.append(store)
    loads[1].wait()
    both = [halves[half].astype(F32).reshape(ROWS, GROUP, HD) for half in range(2)]
    joined[...] = jnp.concatenate(both, axis=1).astype(BF16)
    store = pltpu.make_async_copy(joined, attn_out, sem.at[6])
    store.start()
    stores.append(store)
    loads[2].wait()
    wide_joined[...] = jnp.concatenate(
        [wide[half].reshape(ROWS, GROUP, HD) for half in range(2)], axis=1
    )
    store = pltpu.make_async_copy(wide_joined, dq_out, sem.at[3])
    store.start()
    stores.append(store)
    for store in stores:
        store.wait()


def finish(attn, dq, dkv):
    return pl.pallas_call(
        finish_kernel,
        out_shape=(
            jax.ShapeDtypeStruct((ROWS, 2 * GROUP, HD), BF16),
            jax.ShapeDtypeStruct((ROWS, 2 * GROUP, HD), F32),
            jax.ShapeDtypeStruct((2 * ROWS, HD), F32),
            jax.ShapeDtypeStruct((2 * ROWS, HD), F32),
        ),
        in_specs=[HBM] * 3,
        out_specs=(HBM,) * 4,
        scratch_shapes=[
            pltpu.VMEM((2, ROWS * GROUP, HD), BF16),
            pltpu.VMEM((ROWS, 2 * GROUP, HD), BF16),
            pltpu.VMEM((2, ROWS * GROUP, HD), F32),
            pltpu.VMEM((ROWS, 2 * GROUP, HD), F32),
            pltpu.VMEM((2, 2, ROWS, HD), F32),
            pltpu.VMEM((2 * ROWS, HD), F32),
            pltpu.VMEM((2 * ROWS, HD), F32),
            pltpu.SemaphoreType.DMA((7,)),
        ],
        compiler_params=pltpu.CompilerParams(vmem_limit_bytes=60 << 20),
        cost_estimate=pl.CostEstimate(flops=0, bytes_accessed=4 << 20, transcendentals=0),
        name="finish",
    )(attn, dq, dkv)


def local(queries, keys, values, grad_out, span_order, doc_ids):
    turned = [jnp.transpose(a, (1, 2, 0)) for a in (queries, keys, values, grad_out)]
    q_cols, g_cols, q_rows, g_rows, kv = bring(*turned)
    kv = kv.reshape(2 * NZ, 2, 4, SPAN, HD)
    attn, dq, dkv = attend(
        span_order, doc_ids.reshape(SLOTS, ROWS), q_cols, g_cols, q_rows, g_rows, kv
    )
    attn, dq, dkv = give_back(attn, dq, dkv.reshape(2 * NZ, 2, 2 * ROWS, HD))
    attn, dq, dk, dv = finish(attn, dq, dkv)
    return (attn, dq, dk.reshape(ROWS, 2, HD), dv.reshape(ROWS, 2, HD))


def solution(mesh):
    entry = P(("outer", "inner"), None, "head")
    leave = P(("outer", "inner"), "head", None)
    return jax.shard_map(
        local,
        mesh=mesh,
        in_specs=(entry, entry, entry, entry, P(), P()),
        out_specs=(leave, leave, leave, leave),
        check_vma=False,
    )
```

time: 113 us -> 81.1 us (0.72)
  Pallas kernels: 102 us -> 80.2 us
  local copies, waits for them, and re-layouts: 9.96 us -> 0 us
    pallas_call x2 -> x3, Pallas kernels: 73 us -> 48.3 us  [the longest x1 35.6 us: bring(): pl.pallas_call(bring_kernel, out_shape=(jax.ShapeDtypeStruct((4, HD, LANE...]
    unnamed x16 -> x0, local copies, waits for them, and re-layouts: 8.01 us -> none
    pallas_call x1, Pallas kernels: 29.3 us -> 31.9 us  [give_back(): pl.pallas_call(return_kernel, out_shape=(jax.ShapeDtypeStruct((2, ROWS *...]
    reshape x2 -> x0, local copies, waits for them, and re-layouts: 1.93 us -> none  [join(): return halves.reshape(2, ROWS, GROUP, HD).transpose(1, 0, 2, 3).reshape(R...]
where the time goes in v2:
time: 81.1 us; the launch traced here: 80.9 us
  Pallas kernels  80.2 us (99%)
    pallas_call x1, Pallas kernels, bring(): pl.pallas_call(bring_kernel, out_shape=(jax.ShapeDtypeStruct((4, HD, LANE...  35.6 us
    pallas_call x1, Pallas kernels, give_back(): pl.pallas_call(return_kernel, out_shape=(jax.ShapeDtypeStruct((2, ROWS *...  31.9 us
    pallas_call x1, Pallas kernels, attend(): pl.pallas_call(attend_kernel, out_shape=(jax.ShapeDtypeStruct((4, HD, LAN...  10.1 us
    pallas_call x1, Pallas kernels, finish(): pl.pallas_call(finish_kernel, out_shape=(jax.ShapeDtypeStruct((ROWS, 2 *...  2.57 us

profile of v2, /device:TPU:1, one launch (start us, length us, event | category | flops | bytes accessed | tf_op | source)
XLA Modules:
  0.0 80.9 jit_solution(7912135856142610570)
XLA Ops:
  0.6 35.6 %bring.1 = (bf16[4,128,512]{2,1,0:T(8,128)(2,1)}, bf16[4,128,512]{2,1,0:T(8,128)(2,1)}, bf16[4,512,128]{2,1,0:T(8,128)(2,1)}, bf16[4,512,128]{2,1,0:T(8,128)(2,1)}, bf16[16,2,256,128]{3,2,1,0:T(8,128)(2,1)}) custom-call(bf16[64,32,128]{2,1,0:T(8,128)(2,1)} %bitcast.10, bf16[8,32,128]{2,1,0:T(8,128)(2,1)} %bitcast.12, bf16[8,32,128]{2,1,0:T(8,128)(2,1)} %bitcast.13, ...), custom_call_target="tpu_custom_call" | custom-call | tf_op jit(solution)/shard_map/bring/pallas_call | solution.py:239
  36.2 10.1 %attend.1 = (bf16[4,128,512]{2,1,0:T(8,128)(2,1)}, f32[4,128,512]{2,1,0:T(8,128)}, bf16[16,2,4,64,128]{4,3,2,1,0:T(8,128)(2,1)}) custom-call(s32[128]{0:T(128)} %order_in.1, s32[64,128]{1,0:T(8,128)} %bitcast.17, bf16[4,128,512]{2,1,0:T(8,128)(2,1)} %get-tuple-element.19.q_cols_in, bf16[4,128,512]{2,1,0:T(8,128)(2,1)} %get-tuple-element.20.g_cols_in, ...), custom_call_target="tpu_custom_call" | custom-call | flops 6442450944 | bytes 12582912 | tf_op jit(solution)/shard_map/attend/pallas_call | solution.py:482
  46.4 31.9 %give_back.1 = (bf16[2,1024,128]{2,1,0:T(8,128)(2,1)}, f32[2,1024,128]{2,1,0:T(8,128)}, f32[2,2,128,128]{3,2,1,0:T(8,128)}) custom-call(bf16[4,128,512]{2,1,0:T(8,128)(2,1)} %get-tuple-element.24.attn_in, f32[4,128,512]{2,1,0:T(8,128)} %get-tuple-element.25.dq_in, bf16[16,2,256,128]{3,2,1,0:T(8,128)(2,1)} %bitcast.9), custom_call_target="tpu_custom_call" | custom-call | tf_op jit(solution)/shard_map/give_back/pallas_call | solution.py:682
  78.3 2.6 %finish.1 = (bf16[128,16,128]{2,1,0:T(8,128)(2,1)}, f32[128,16,128]{2,1,0:T(8,128)}, f32[256,128]{1,0:T(8,128)}, f32[256,128]{1,0:T(8,128)}) custom-call(bf16[2,1024,128]{2,1,0:T(8,128)(2,1)} %get-tuple-element.27.attn, f32[2,1024,128]{2,1,0:T(8,128)} %get-tuple-element.28.dq, f32[2,2,128,128]{3,2,1,0:T(8,128)} %get-tuple-element.29.dkv), custom_call_target="tpu_custom_call" | custom-call | bytes 4194304 | tf_op jit(solution)/shard_map/finish/pallas_call | solution.py:749

commit v3 on v2

--- a/solution.py
+++ b/solution.py
@@ -64,7 +64,7 @@
 
 def bring_kernel(
     q, k, v, g, q_cols_out, g_cols_out, q_rows_out, g_rows_out, kv_out,
-    q_cols, g_cols, q_rows, g_rows, out_sem, q_in, g_in, kv_in, ring_kv, own_sem, keep_sem, x_send, x_recv, y_send, y_recv, z_send, z_recv,
+    q_cols, g_cols, q_rows, g_rows, out_sem, q_in, g_in, kv_in, ring_kv, relay, relay_sem, own_sem, keep_sem, x_send, x_recv, y_send, y_recv, z_send, z_recv,
 ):
     x, y, z, core = place()
     peers = [(dx, dc) for dx in range(NX) for dc in range(2) if (dx, dc) != (0, 0)]
@@ -128,7 +128,7 @@
         block = block_at(0, way, step)
         copy = send(
             ring_kv.at[block, kind], ring_kv.at[NZ + block, kind],
-            y_send.at[way, step // 2, kind], y_recv.at[way, step // 2, kind], later,
+            y_send.at[way, step, kind], y_recv.at[way, step, kind], later,
         )
         sent.append(copy)
         return copy
@@ -176,8 +176,18 @@
         copy.start()
         own.append(copy)
     wide = ([], [])
+    relays = []
+    for kind, src in enumerate((q, g)):
+        relays.append(
+            send(
+                src.at[pl.ds(lax.rem(x + 2, NX) * 2 * GROUP, 2 * GROUP)], relay.at[kind],
+                relay_sem.at[0, kind], relay_sem.at[1, kind], peer(3 if kind else 1, 0),
+            )
+        )
     for kind, (src, dst) in enumerate(((q, q_in), (g, g_in))):
         for index, (dx, dc) in enumerate(peers):
+            if dx == 2:
+                continue
             head = lax.rem(x + dx, NX) * 2 + lax.rem(core + dc, 2)
             wide[kind].append(
                 send(
@@ -188,6 +198,24 @@
                     peer(dx, dc),
                 )
             )
+    def forward(kind):
+        relays[kind].wait_recv()
+        from_x = lax.rem(x + (1 if kind else 3), NX)
+        there = pl.ds(pl.multiple_of(from_x * 32, 32), 32)
+        for index, (dx, dc) in enumerate(peers):
+            if dx != 2:
+                continue
+            head = pl.ds(lax.rem(core + dc, 2) * GROUP, GROUP)
+            wide[kind].append(
+                send(
+                    relay.at[kind, head],
+                    (q_in, g_in)[kind].at[core, :, there],
+                    x_send.at[2 + kind, index],
+                    x_recv.at[2 + kind, index],
+                    peer(3 if kind else 1, dc),
+                )
+            )
+
     far_shift = {}
     for step in range(1, 4):
         for kind in range(2):
@@ -195,15 +223,17 @@
                 near[way, step, kind].wait_recv()
                 if step < 3 or kind == way:
                     near[way, step + 1, kind] = hop(0, way, step + 1, kind)
-                if step == 2:
-                    far_shift[way, kind] = shift(way, 2, kind)
+                if step == 2 or (step == 1 and kind == way):
+                    far_shift[way, step, kind] = shift(way, step, kind)
         for way in range(2):
             keep(block_at(0, way, step), 1 + 2 * step + way)
+        if step == 1:
+            forward(0)
+            forward(1)
     hops = {}
     for kind in range(2):
         self_shift[kind].wait_recv()
-        for way in range(2):
-            hops[way, 1, kind] = hop(1, way, 1, kind)
+        hops[1 - kind, 1, kind] = hop(1, 1 - kind, 1, kind)
     keep(NZ + z, 1)
     last_shift = []
     for way in range(2):
@@ -212,7 +242,7 @@
     keep(block_at(0, 0, 4), 2)
     for kind in range(2):
         for way in range(2):
-            far_shift[way, kind].wait_recv()
+            far_shift[way, 2, kind].wait_recv()
             hops[way, 3, kind] = hop(1, way, 3, kind)
     for way in range(2):
         keep(block_at(1, way, 2), 9 + way)
@@ -220,14 +250,15 @@
     for step in (1, 3):
         for way in range(2):
             for kind in range(2):
-                hops[way, step, kind].wait_recv()
+                arriving = far_shift if step == 1 and kind == way else hops
+                arriving[way, step, kind].wait_recv()
             keep(block_at(1, way, step), 10 + step + way)
         if step == 1:
             for way in range(2):
                 last_shift[way].wait_recv()
             keep(block_at(1, 0, 4), 15)
             settle(1)
-    for copy in sent:
+    for copy in sent + relays:
         copy.wait_send()
     for copy in keeps:
         copy.wait()
@@ -257,12 +288,14 @@
             pltpu.VMEM((2, GROUP, HD, ROWS), BF16),
             pltpu.VMEM((2, 2, HD, ROWS), BF16),
             pltpu.VMEM((2 * NZ, 2, 2 * ROWS, HD), BF16),
+            pltpu.VMEM((2, 2 * GROUP, HD // NX, ROWS), BF16),
+            pltpu.SemaphoreType.DMA((2, 2)),
             pltpu.SemaphoreType.DMA((4,)),
             pltpu.SemaphoreType.DMA((16,)),
             pltpu.SemaphoreType.DMA((4, 8)),
             pltpu.SemaphoreType.DMA((4, 8)),
-            pltpu.SemaphoreType.DMA((2, 3, 2)),
-            pltpu.SemaphoreType.DMA((2, 3, 2)),
+            pltpu.SemaphoreType.DMA((2, 5, 2)),
+            pltpu.SemaphoreType.DMA((2, 5, 2)),
             pltpu.SemaphoreType.DMA((2, 2, 4, 2)),
             pltpu.SemaphoreType.DMA((2, 2, 4, 2)),
         ],
@@ -275,7 +308,7 @@
 
 def attend_kernel(
     order_in, docs_in, q_cols_in, g_cols_in, q_rows_in, g_rows_in, kv_in, attn_out, dq_out, dkv,
-    order, docs, q_cols, g_cols, q_rows, g_rows, attn, dq, kv, scores, key_acc, value_acc, out_acc, tops, sums, shift, dots,
+    order, docs, q_cols, g_cols, q_rows, g_rows, attn, dq, kv, scores, key_acc, value_acc, out_acc, tops, sums, shift, dots, grads,
     pos_rows, start_rows, item_list, span_list, in_sem, out_sem,
 ):
     outer = lax.axis_index("outer")
@@ -292,10 +325,6 @@
     ]
     for load in loads:
         load.start()
-    key_acc[...] = jnp.zeros_like(key_acc)
-    value_acc[...] = jnp.zeros_like(value_acc)
-    out_acc[...] = jnp.zeros_like(out_acc)
-    dq[...] = jnp.zeros_like(dq)
     tops[...] = jnp.full_like(tops, NEG)
     sums[...] = jnp.zeros_like(sums)
     loads[0].wait()
@@ -337,6 +366,14 @@
                     allowed = (span >= lows[unit]) & (span <= highs[unit])
                     new.append(counts[unit] + jnp.where(allowed, 1, 0))
                 counts = tuple(new)
+            nothing = jnp.zeros((8, SPAN, HD), F32)
+            rows = pl.ds(pl.multiple_of((group * 4 + step) * 8, 8), 8)
+            key_acc[rows] = nothing
+            value_acc[rows] = nothing
+            flat = pl.ds(pl.multiple_of(step * 32, 32), 32)
+            for unit in range(2 * group, 2 * group + 2):
+                out_acc[unit, flat, :] = jnp.zeros((32, LANES), F32)
+                dq[unit, flat, :] = jnp.zeros((32, LANES), F32)
             return counts
 
         counts = lax.fori_loop(0, 4, note, counts)
@@ -350,8 +387,10 @@
     blank = 3 * 128 + 72
     for extra in range(ITEM):
         span_list[blank + extra] = FAR
-    item_list[items] = blank
+    for extra in range(4):
+        item_list[items + extra] = blank
     steps = lax.div(items + 1, 2)
+    long_steps = lax.div(items + 3, 4)
 
     iota_keys = (
         lax.broadcasted_iota(jnp.int32, (8, 8, ROWS), 0) * 8
@@ -374,10 +413,10 @@
     loads[2].wait()
     loads[3].wait()
 
-    @functools.partial(lax.fori_loop, 0, steps, init_val=0)
+    @functools.partial(lax.fori_loop, 0, long_steps, init_val=0)
     def _(step, _):
         results = []
-        for item in (2 * step, 2 * step + 1):
+        for item in [4 * step + part for part in range(4)]:
             unit, slots, bases = entries(item)
             keys = spans(slots, 0)
             biases = []
@@ -401,10 +440,10 @@
         shift[unit] = jnp.broadcast_to(jnp.max(tops[unit], axis=0, keepdims=True), (8, LANES))
     loads[4].wait()
 
-    @functools.partial(lax.fori_loop, 0, steps, init_val=0)
+    @functools.partial(lax.fori_loop, 0, long_steps, init_val=0)
     def _(step, _):
         results = []
-        for item in (2 * step, 2 * step + 1):
+        for item in [4 * step + part for part in range(4)]:
             unit, slots, _ = entries(item)
             values_t = spans(slots, 1).T
             for lanes in sides:
@@ -433,23 +472,38 @@
     attn_store = pltpu.make_async_copy(attn, attn_out, out_sem.at[2 * NZ])
     attn_store.start()
 
+    def ahead(step):
+        half = lax.rem(step, 2)
+        for part in range(2):
+            unit, slots, _ = entries(2 * step + part)
+            values = spans(slots, 1)
+            for lanes in sides:
+                grads[half, part, :, lanes] = jnp.dot(
+                    values, g_cols[unit, :, lanes], preferred_element_type=F32
+                )
+
+    ahead(0)
+
     @functools.partial(lax.fori_loop, 0, steps, init_val=0)
     def _(step, _):
         results = []
-        for item in (2 * step, 2 * step + 1):
+        mine = []
+        for part in range(2):
+            item = 2 * step + part
             unit, slots, _ = entries(item)
-            keys = spans(slots, 0)
-            values = spans(slots, 1)
-            keys_t = keys.T
             probs_b = []
             score_grads = []
             for lanes in sides:
                 logits = scores[item, :, lanes].reshape(32, 8, 256)
                 probs = jnp.exp2(logits - shift[unit, :, lanes][None])
-                grads = jnp.dot(values, g_cols[unit, :, lanes], preferred_element_type=F32)
-                grads = probs * (grads.reshape(32, 8, 256) - dots[unit, :, lanes][None])
+                steep = grads[lax.rem(step, 2), part, :, lanes].reshape(32, 8, 256)
+                steep = probs * (steep - dots[unit, :, lanes][None])
                 probs_b.append(probs.reshape(256, 256).astype(BF16))
-                score_grads.append(grads.reshape(256, 256).astype(BF16))
+                score_grads.append(steep.reshape(256, 256).astype(BF16))
+            mine.append((unit, slots, probs_b, score_grads))
+        ahead(step + 1)
+        for unit, slots, probs_b, score_grads in mine:
+            keys_t = spans(slots, 0).T
             probs_b = jnp.concatenate(probs_b, axis=1)
             score_grads = jnp.concatenate(score_grads, axis=1)
             to_values = jnp.dot(probs_b, g_rows[unit], preferred_element_type=F32)
@@ -506,6 +560,7 @@
             pltpu.VMEM((4, 8, LANES), F32),
             pltpu.VMEM((4, 8, LANES), F32),
             pltpu.VMEM((4, 8, LANES), F32),
+            pltpu.VMEM((2, 2, ITEM * SPAN, LANES), F32),
             pltpu.VMEM((4, 8, ROWS), jnp.int32),
             pltpu.VMEM((4, 8, ROWS), jnp.int32),
             pltpu.SMEM((80,), jnp.int32),
@@ -561,6 +616,8 @@
     for step, distance in ((0, 3), (1, 1)):
         for kind in range(2):
             for way in range(2):
+                if step == 1 and kind == way:
+                    continue
                 flying["z", step, way, kind] = ship(
                     dkv.at[at(1, distance, way), kind], step * 4 + way * 2 + kind, ways[way]
                 )
@@ -608,6 +665,8 @@
             flying["y", 2, way, kind] = ship(
                 terms.at[block, kind], 10 + way * 2 + kind, earlier
             )
+    for way in range(2):
+        flying["y", 1, way] = ship(dkv.at[at(1, 1, way), way], 30 + way, earlier)
     for way in range(2):
         flying["y", 4, way].wait_recv()
         block = at(0, 4, 0)
@@ -628,9 +687,9 @@
             terms.at[at(0, 3, way), way], 18 + way * 2 + way, ways[way]
         )
     for kind in range(2):
-        for way in range(2):
-            flying["z", 1, way, kind].wait_recv()
-        add(NZ + z, kind, 4 + kind, 6 + kind)
+        way = 1 - kind
+        flying["z", 1, way, kind].wait_recv()
+        add(NZ + z, kind, 4 + way * 2 + kind)
         flying["y", 0, kind] = ship(terms.at[NZ + z, kind], 14 + kind, earlier)
     for step in (3, 4):
         for turn_of in range(2):
@@ -641,6 +700,9 @@
                 if step == 3:
                     flying["y", 2, way, kind].wait_recv()
                     indices.append(10 + way * 2 + kind)
+                elif kind == way:
+                    flying["y", 1, way].wait_recv()
+                    indices.append(30 + way)
                 block = at(0, 5 - step, way)
                 add(block, kind, *indices)
                 flying["s", step, way, kind] = ship(
@@ -695,13 +757,13 @@
             pltpu.VMEM((2, ROWS * GROUP, HD), BF16),
             pltpu.VMEM((2, ROWS * GROUP, HD), F32),
             pltpu.VMEM((LANES, HD), F32),
-            pltpu.VMEM((30, 2 * ROWS, HD), BF16),
+            pltpu.VMEM((32, 2 * ROWS, HD), BF16),
             pltpu.VMEM((2, 2 * ROWS, HD), F32),
             pltpu.SemaphoreType.DMA((4,)),
             pltpu.SemaphoreType.DMA((4,)),
             pltpu.SemaphoreType.DMA((7,)),
-            pltpu.SemaphoreType.DMA((30,)),
-            pltpu.SemaphoreType.DMA((30,)),
+            pltpu.SemaphoreType.DMA((32,)),
+            pltpu.SemaphoreType.DMA((32,)),
         ],
         compiler_params=pltpu.CompilerParams(
             collective_id=1, has_side_effects=True, vmem_limit_bytes=60 << 20

time: 81.1 us -> 88.6 us (1.092)
  Pallas kernels: 80.2 us -> 87.7 us
    pallas_call x1, Pallas kernels: 31.9 us -> 38.7 us  [give_back(): pl.pallas_call(return_kernel, out_shape=(jax.ShapeDtypeStruct((2, ROWS *...]
    pallas_call x1, Pallas kernels: 10.1 us -> 11.3 us  [attend(): pl.pallas_call(attend_kernel, out_shape=(jax.ShapeDtypeStruct((4, HD, LAN...]
where the time goes in v3:
time: 88.6 us; the launch traced here: 88.3 us
  Pallas kernels  87.7 us (99%)
    pallas_call x1, Pallas kernels, give_back(): pl.pallas_call(return_kernel, out_shape=(jax.ShapeDtypeStruct((2, ROWS *...  38.7 us
    pallas_call x1, Pallas kernels, bring(): pl.pallas_call(bring_kernel, out_shape=(jax.ShapeDtypeStruct((4, HD, LANE...  35.2 us
    pallas_call x1, Pallas kernels, attend(): pl.pallas_call(attend_kernel, out_shape=(jax.ShapeDtypeStruct((4, HD, LAN...  11.3 us
    pallas_call x1, Pallas kernels, finish(): pl.pallas_call(finish_kernel, out_shape=(jax.ShapeDtypeStruct((ROWS, 2 *...  2.57 us

profile of v3, /device:TPU:1, one launch (start us, length us, event | category | flops | bytes accessed | tf_op | source)
XLA Modules:
  0.0 88.3 jit_solution(2576347674158838149)
XLA Ops:
  0.6 35.2 %bring.1 = (bf16[4,128,512]{2,1,0:T(8,128)(2,1)}, bf16[4,128,512]{2,1,0:T(8,128)(2,1)}, bf16[4,512,128]{2,1,0:T(8,128)(2,1)}, bf16[4,512,128]{2,1,0:T(8,128)(2,1)}, bf16[16,2,256,128]{3,2,1,0:T(8,128)(2,1)}) custom-call(bf16[64,32,128]{2,1,0:T(8,128)(2,1)} %bitcast.10, bf16[8,32,128]{2,1,0:T(8,128)(2,1)} %bitcast.12, bf16[8,32,128]{2,1,0:T(8,128)(2,1)} %bitcast.13, ...), custom_call_target="tpu_custom_call" | custom-call | tf_op jit(solution)/shard_map/bring/pallas_call | solution.py:270
  35.8 11.3 %attend.1 = (bf16[4,128,512]{2,1,0:T(8,128)(2,1)}, f32[4,128,512]{2,1,0:T(8,128)}, bf16[16,2,4,64,128]{4,3,2,1,0:T(8,128)(2,1)}) custom-call(s32[128]{0:T(128)} %order_in.1, s32[64,128]{1,0:T(8,128)} %bitcast.17, bf16[4,128,512]{2,1,0:T(8,128)(2,1)} %get-tuple-element.19.q_cols_in, bf16[4,128,512]{2,1,0:T(8,128)(2,1)} %get-tuple-element.20.g_cols_in, ...), custom_call_target="tpu_custom_call" | custom-call | flops 6442450944 | bytes 12582912 | tf_op jit(solution)/shard_map/attend/pallas_call | solution.py:536
  47.1 38.7 %give_back.1 = (bf16[2,1024,128]{2,1,0:T(8,128)(2,1)}, f32[2,1024,128]{2,1,0:T(8,128)}, f32[2,2,128,128]{3,2,1,0:T(8,128)}) custom-call(bf16[4,128,512]{2,1,0:T(8,128)(2,1)} %get-tuple-element.24.attn_in, f32[4,128,512]{2,1,0:T(8,128)} %get-tuple-element.25.dq_in, bf16[16,2,256,128]{3,2,1,0:T(8,128)(2,1)} %bitcast.9), custom_call_target="tpu_custom_call" | custom-call | tf_op jit(solution)/shard_map/give_back/pallas_call | solution.py:744
  85.8 2.6 %finish.1 = (bf16[128,16,128]{2,1,0:T(8,128)(2,1)}, f32[128,16,128]{2,1,0:T(8,128)}, f32[256,128]{1,0:T(8,128)}, f32[256,128]{1,0:T(8,128)}) custom-call(bf16[2,1024,128]{2,1,0:T(8,128)(2,1)} %get-tuple-element.27.attn, f32[2,1024,128]{2,1,0:T(8,128)} %get-tuple-element.28.dq, f32[2,2,128,128]{3,2,1,0:T(8,128)} %get-tuple-element.29.dkv), custom_call_target="tpu_custom_call" | custom-call | bytes 4194304 | tf_op jit(solution)/shard_map/finish/pallas_call | solution.py:811

commit v4 on v3

--- a/solution.py
+++ b/solution.py
@@ -76,7 +76,11 @@
     down = where_is(x, y, lax.rem(z + NZ - 1, NZ), core)
     later = where_is(x, lax.rem(y + 1, NY), z, core)
     earlier = where_is(x, lax.rem(y + NY - 1, NY), z, core)
-    greet([peer(*p) for p in peers] + [up, down, later, earlier])
+    up_z, down_z = lax.rem(z + 1, NZ), lax.rem(z + NZ - 1, NZ)
+    later_y, earlier_y = lax.rem(y + 1, NY), lax.rem(y + NY - 1, NY)
+    corners = (where_is(x, later_y, up_z, core), where_is(x, later_y, down_z, core))
+    behind = [where_is(x, earlier_y, up_z, core), where_is(x, earlier_y, down_z, core)]
+    greet([peer(*p) for p in peers] + [up, down, later, earlier, *corners, *behind])
 
     here = pl.ds(pl.multiple_of(x * 32, 32), 32)
     copies = []
@@ -125,10 +129,11 @@
         return copy
 
     def shift(way, step, kind):
-        block = block_at(0, way, step)
+        block = block_at(0, way, min(step, 3))
         copy = send(
             ring_kv.at[block, kind], ring_kv.at[NZ + block, kind],
-            y_send.at[way, step, kind], y_recv.at[way, step, kind], later,
+            y_send.at[way, step, kind], y_recv.at[way, step, kind],
+            corners[way] if step == 4 else later,
         )
         sent.append(copy)
         return copy
@@ -223,6 +228,8 @@
                 near[way, step, kind].wait_recv()
                 if step < 3 or kind == way:
                     near[way, step + 1, kind] = hop(0, way, step + 1, kind)
+                if step == 3 and kind == way:
+                    far_shift[way, 4] = shift(way, 4, way)
                 if step == 2 or (step == 1 and kind == way):
                     far_shift[way, step, kind] = shift(way, step, kind)
         for way in range(2):
@@ -235,11 +242,6 @@
         self_shift[kind].wait_recv()
         hops[1 - kind, 1, kind] = hop(1, 1 - kind, 1, kind)
     keep(NZ + z, 1)
-    last_shift = []
-    for way in range(2):
-        near[way, 4, way].wait_recv()
-        last_shift.append(shift(way, 4, way))
-    keep(block_at(0, 0, 4), 2)
     for kind in range(2):
         for way in range(2):
             far_shift[way, 2, kind].wait_recv()
@@ -247,17 +249,19 @@
     for way in range(2):
         keep(block_at(1, way, 2), 9 + way)
     settle(0)
+    settle(1)
+    for way in range(2):
+        near[way, 4, way].wait_recv()
+    keep(block_at(0, 0, 4), 2)
     for step in (1, 3):
         for way in range(2):
             for kind in range(2):
                 arriving = far_shift if step == 1 and kind == way else hops
                 arriving[way, step, kind].wait_recv()
             keep(block_at(1, way, step), 10 + step + way)
-        if step == 1:
-            for way in range(2):
-                last_shift[way].wait_recv()
-            keep(block_at(1, 0, 4), 15)
-            settle(1)
+    for way in range(2):
+        far_shift[way, 4].wait_recv()
+    keep(block_at(1, 0, 4), 15)
     for copy in sent + relays:
         copy.wait_send()
     for copy in keeps:
@@ -308,7 +312,7 @@
 
 def attend_kernel(
     order_in, docs_in, q_cols_in, g_cols_in, q_rows_in, g_rows_in, kv_in, attn_out, dq_out, dkv,
-    order, docs, q_cols, g_cols, q_rows, g_rows, attn, dq, kv, scores, key_acc, value_acc, out_acc, tops, sums, shift, dots, grads,
+    order, docs, q_cols, g_cols, q_rows, g_rows, attn, dq, kv, scores, key_acc, value_acc, out_acc, tops, sums, shift, dots,
     pos_rows, start_rows, item_list, span_list, in_sem, out_sem,
 ):
     outer = lax.axis_index("outer")
@@ -317,14 +321,15 @@
         pltpu.make_async_copy(order_in, order, in_sem.at[0]),
         pltpu.make_async_copy(docs_in, docs, in_sem.at[1]),
         pltpu.make_async_copy(q_cols_in, q_cols, in_sem.at[2]),
-        pltpu.make_async_copy(kv_in.at[:, 0], kv.at[:, 0], in_sem.at[3]),
-        pltpu.make_async_copy(kv_in.at[:, 1], kv.at[:, 1], in_sem.at[4]),
+        pltpu.make_async_copy(kv_in.at[:, 0], kv.at[pl.ds(0, 2 * NZ), 0], in_sem.at[3]),
+        pltpu.make_async_copy(kv_in.at[:, 1], kv.at[pl.ds(0, 2 * NZ), 1], in_sem.at[4]),
         pltpu.make_async_copy(g_cols_in, g_cols, in_sem.at[5]),
         pltpu.make_async_copy(q_rows_in, q_rows, in_sem.at[6]),
         pltpu.make_async_copy(g_rows_in, g_rows, in_sem.at[7]),
     ]
     for load in loads:
         load.start()
+    kv[2 * NZ] = jnp.zeros((2, 4, SPAN, HD), BF16)
     tops[...] = jnp.full_like(tops, NEG)
     sums[...] = jnp.zeros_like(sums)
     loads[0].wait()
@@ -359,7 +364,7 @@
             for part in range(8):
                 slot = step * 8 + part
                 span = order[stored + slot]
-                entry = span * SPAN + (group * 32 + slot)
+                entry = span * (2 * SPAN) + (group * 32 + slot)
                 new = []
                 for unit in range(4):
                     span_list[counts[unit]] = entry
@@ -367,7 +372,7 @@
                     new.append(counts[unit] + jnp.where(allowed, 1, 0))
                 counts = tuple(new)
             nothing = jnp.zeros((8, SPAN, HD), F32)
-            rows = pl.ds(pl.multiple_of((group * 4 + step) * 8, 8), 8)
+            rows = pl.ds((group * 4 + step) * 8, 8)
             key_acc[rows] = nothing
             value_acc[rows] = nothing
             flat = pl.ds(pl.multiple_of(step * 32, 32), 32)
@@ -380,13 +385,13 @@
     items = jnp.int32(0)
     for unit in range(4):
         for extra in range(ITEM):
-            span_list[counts[unit] + extra] = FAR
+            span_list[counts[unit] + extra] = 2 * FAR + SLOTS
         for chunk in range(SLOTS // ITEM):
             item_list[items + chunk] = unit * 128 + chunk * ITEM
         items = items + lax.div(counts[unit] - unit * 128 + ITEM - 1, ITEM)
     blank = 3 * 128 + 72
     for extra in range(ITEM):
-        span_list[blank + extra] = FAR
+        span_list[blank + extra] = 2 * FAR + SLOTS
     for extra in range(4):
         item_list[items + extra] = blank
     steps = lax.div(items + 1, 2)
@@ -400,8 +405,8 @@
     def entries(item):
         first = item_list[item]
         found = [span_list[first + part] for part in range(ITEM)]
-        slots = [lax.rem(entry, SLOTS) for entry in found]
-        return lax.div(first, 128), slots, [a - b for a, b in zip(found, slots)]
+        slots = [lax.rem(entry, 2 * SPAN) for entry in found]
+        return lax.div(first, 128), slots, [lax.div(a - b, 2) for a, b in zip(found, slots)]
 
     def spans(slots, kind):
         parts = []
@@ -472,38 +477,22 @@
     attn_store = pltpu.make_async_copy(attn, attn_out, out_sem.at[2 * NZ])
     attn_store.start()
 
-    def ahead(step):
-        half = lax.rem(step, 2)
-        for part in range(2):
-            unit, slots, _ = entries(2 * step + part)
-            values = spans(slots, 1)
-            for lanes in sides:
-                grads[half, part, :, lanes] = jnp.dot(
-                    values, g_cols[unit, :, lanes], preferred_element_type=F32
-                )
-
-    ahead(0)
-
     @functools.partial(lax.fori_loop, 0, steps, init_val=0)
     def _(step, _):
         results = []
-        mine = []
-        for part in range(2):
-            item = 2 * step + part
+        for item in (2 * step, 2 * step + 1):
             unit, slots, _ = entries(item)
+            keys_t = spans(slots, 0).T
+            values = spans(slots, 1)
             probs_b = []
             score_grads = []
             for lanes in sides:
                 logits = scores[item, :, lanes].reshape(32, 8, 256)
                 probs = jnp.exp2(logits - shift[unit, :, lanes][None])
-                steep = grads[lax.rem(step, 2), part, :, lanes].reshape(32, 8, 256)
-                steep = probs * (steep - dots[unit, :, lanes][None])
+                steep = jnp.dot(values, g_cols[unit, :, lanes], preferred_element_type=F32)
+                steep = probs * (steep.reshape(32, 8, 256) - dots[unit, :, lanes][None])
                 probs_b.append(probs.reshape(256, 256).astype(BF16))
                 score_grads.append(steep.reshape(256, 256).astype(BF16))
-            mine.append((unit, slots, probs_b, score_grads))
-        ahead(step + 1)
-        for unit, slots, probs_b, score_grads in mine:
-            keys_t = spans(slots, 0).T
             probs_b = jnp.concatenate(probs_b, axis=1)
             score_grads = jnp.concatenate(score_grads, axis=1)
             to_values = jnp.dot(probs_b, g_rows[unit], preferred_element_type=F32)
@@ -512,10 +501,13 @@
             results.append((slots, unit, to_values, to_keys, to_query))
         for slots, unit, to_values, to_keys, to_query in results:
             dq[unit] += to_query
-            for part, slot in enumerate(slots):
-                rows = slice(part * SPAN, (part + 1) * SPAN)
-                key_acc[slot] += to_keys[rows]
-                value_acc[slot] += to_values[rows]
+            for acc, part in ((key_acc, to_keys), (value_acc, to_values)):
+                sums_of = [
+                    acc[slot] + part[index * SPAN : (index + 1) * SPAN]
+                    for index, slot in enumerate(slots)
+                ]
+                for slot, total in zip(slots, sums_of):
+                    acc[slot] = total
         return 0
 
     dq_store = pltpu.make_async_copy(dq, dq_out, out_sem.at[2 * NZ + 1])
@@ -551,16 +543,15 @@
             pltpu.VMEM((4, LANES, HD), BF16),
             pltpu.VMEM((4, HD, LANES), BF16),
             pltpu.VMEM((4, HD, LANES), F32),
-            pltpu.VMEM((2 * NZ, 2, 4, SPAN, HD), BF16),
+            pltpu.VMEM((2 * NZ + 1, 2, 4, SPAN, HD), BF16),
             pltpu.VMEM((4 * SLOTS // ITEM, ITEM * SPAN, LANES), F32),
-            pltpu.VMEM((SLOTS, SPAN, HD), F32),
-            pltpu.VMEM((SLOTS, SPAN, HD), F32),
+            pltpu.VMEM((SLOTS + 1, SPAN, HD), F32),
+            pltpu.VMEM((SLOTS + 1, SPAN, HD), F32),
             pltpu.VMEM((4, HD, LANES), F32),
             pltpu.VMEM((4, 8, LANES), F32),
             pltpu.VMEM((4, 8, LANES), F32),
             pltpu.VMEM((4, 8, LANES), F32),
             pltpu.VMEM((4, 8, LANES), F32),
-            pltpu.VMEM((2, 2, ITEM * SPAN, LANES), F32),
             pltpu.VMEM((4, 8, ROWS), jnp.int32),
             pltpu.VMEM((4, 8, ROWS), jnp.int32),
             pltpu.SMEM((80,), jnp.int32),
@@ -578,7 +569,7 @@
 
 def return_kernel(
     attn_in, dq_in, dkv, attn_out, dq_out, dkv_out,
-    attn, dq, terms, attn_rows, dq_rows, rows_tmp, landed, final, pair_send, pair_recv, own_sem, l_send, l_recv,
+    attn, dq, terms, attn_rows, dq_rows, rows_tmp, landed, landed_rows, final, pair_send, pair_recv, own_sem, l_send, l_recv, r_send, r_recv,
 ):
     x, y, z, core = place()
     sibling = where_is(x, y, z, 1 - core)
@@ -593,7 +584,19 @@
     ]
     for load in loads:
         load.start()
-    greet([sibling, up, down, later, earlier])
+    up_z, down_z = lax.rem(z + 1, NZ), lax.rem(z + NZ - 1, NZ)
+    later_y, earlier_y = lax.rem(y + 1, NY), lax.rem(y + NY - 1, NY)
+    corners = (where_is(x, earlier_y, up_z, core), where_is(x, earlier_y, down_z, core))
+    behind = [where_is(x, later_y, up_z, core), where_is(x, later_y, down_z, core)]
+    across = [
+        where_is(x, y, up_z, 1 - core),
+        where_is(x, y, down_z, 1 - core),
+        where_is(x, earlier_y, z, 1 - core),
+    ]
+    greet(
+        [sibling, up, down, later, earlier, *corners, *behind, *across]
+        + [where_is(x, later_y, z, 1 - core)]
+    )
 
     ways = (up, down)
     sent = []
@@ -612,7 +615,23 @@
             total = total + landed[index].astype(F32)
         terms[block, kind] = total.astype(BF16)
 
+    mine = pl.ds(pl.multiple_of(core * ROWS, ROWS), ROWS)
+    other = pl.ds(pl.multiple_of((1 - core) * ROWS, ROWS), ROWS)
+
+    def deliver(block, kind, index, straight, crossed):
+        copies = []
+        for half, rows, partner in ((0, mine, straight), (1, other, crossed)):
+            copy = send(
+                terms.at[block, kind, rows], landed_rows.at[half, index],
+                r_send.at[half, index], r_recv.at[half, index], partner,
+            )
+            sent.append(copy)
+            copies.append(copy)
+        return copies
+
     flying = {}
+    for way in range(2):
+        flying["s", 1, way, way] = ship(dkv.at[at(0, 4, 0), way], 16 + way, ways[way])
     for step, distance in ((0, 3), (1, 1)):
         for kind in range(2):
             for way in range(2):
@@ -623,7 +642,7 @@
                 )
         if step == 0:
             for kind in range(2):
-                flying["y", 4, kind] = ship(dkv.at[at(1, 4, 0), kind], 8 + kind, earlier)
+                flying["y", 4, kind] = ship(dkv.at[at(1, 4, 0), kind], 8 + kind, corners[kind])
     swaps = []
     own = []
 
@@ -668,11 +687,6 @@
     for way in range(2):
         flying["y", 1, way] = ship(dkv.at[at(1, 1, way), way], 30 + way, earlier)
     for way in range(2):
-        flying["y", 4, way].wait_recv()
-        block = at(0, 4, 0)
-        add(block, way, 8 + way)
-        flying["s", 1, way, way] = ship(terms.at[block, way], 16 + way, ways[way])
-    for way in range(2):
         kind = 1 - way
         flying["s", 2, way, kind] = ship(
             terms.at[at(0, 3, way), kind], 18 + way * 2 + kind, ways[way]
@@ -680,9 +694,17 @@
     loads[0].wait()
     loads[1].wait()
     swap()
+    for kind in range(2):
+        swaps.append(
+            send(
+                dkv.at[z, kind, other], landed_rows.at[1, 6 + kind],
+                r_send.at[1, 6 + kind], r_recv.at[1, 6 + kind], sibling,
+            )
+        )
     for way in range(2):
         flying["s", 1, way, way].wait_recv()
-        add(at(0, 3, way), way, 16 + way)
+        flying["y", 4, way].wait_recv()
+        add(at(0, 3, way), way, 16 + way, 8 + way)
         flying["s", 2, way, way] = ship(
             terms.at[at(0, 3, way), way], 18 + way * 2 + way, ways[way]
         )
@@ -690,7 +712,7 @@
         way = 1 - kind
         flying["z", 1, way, kind].wait_recv()
         add(NZ + z, kind, 4 + way * 2 + kind)
-        flying["y", 0, kind] = ship(terms.at[NZ + z, kind], 14 + kind, earlier)
+        flying["y", 0, kind] = deliver(NZ + z, kind, kind, earlier, across[2])
     for step in (3, 4):
         for turn_of in range(2):
             for way in range(2):
@@ -705,37 +727,42 @@
                     indices.append(30 + way)
                 block = at(0, 5 - step, way)
                 add(block, kind, *indices)
-                flying["s", step, way, kind] = ship(
-                    terms.at[block, kind], 18 + (step - 2) * 4 + way * 2 + kind, ways[way]
-                )
+                if step == 3:
+                    flying["s", step, way, kind] = ship(
+                        terms.at[block, kind], 22 + way * 2 + kind, ways[way]
+                    )
+                else:
+                    flying["s", step, way, kind] = deliver(
+                        block, kind, 2 + way * 2 + kind, ways[way], across[way]
+                    )
         if step == 3:
             stay()
     for kind in range(2):
-        flying["y", 0, kind].wait_recv()
-        for way in range(2):
-            flying["s", 4, way, kind].wait_recv()
-        total = terms[z, kind].astype(F32)
-        for index in (14 + kind, 26 + kind, 28 + kind):
-            total = total + landed[index].astype(F32)
-        final[kind] = total
-    mine = pl.ds(pl.multiple_of(core * ROWS, ROWS), ROWS)
-    other = pl.ds(pl.multiple_of((1 - core) * ROWS, ROWS), ROWS)
-    for kind in range(2):
-        swaps.append(
-            send(
-                final.at[kind, other], dkv_out.at[kind, core],
-                pair_send.at[2 + kind], pair_recv.at[2 + kind], sibling,
-            )
-        )
-        copy = pltpu.make_async_copy(
-            final.at[kind, mine], dkv_out.at[kind, core], own_sem.at[2 + kind]
-        )
-        copy.start()
-        own.append(copy)
+        for half in range(2):
+            flying["y", 0, kind][half].wait_recv()
+            for way in range(2):
+                flying["s", 4, way, kind][half].wait_recv()
+            if half:
+                swaps[2 + kind].wait_recv()
+                total = landed_rows[1, 6 + kind].astype(F32)
+            else:
+                total = terms[z, kind, mine].astype(F32)
+            for index in (kind, 2 + kind, 4 + kind):
+                total = total + landed_rows[half, index].astype(F32)
+            final[kind, half] = total
+        for half in range(2):
+            copy = pltpu.make_async_copy(
+                final.at[kind, half], dkv_out.at[kind, core if half == 0 else 1 - core],
+                own_sem.at[2 + (0, 5)[half] + kind],
+            )
+            copy.start()
+            own.append(copy)
     for copy in sent:
         copy.wait_send()
-    for copy in swaps:
+    for copy in swaps[:2]:
         copy.wait()
+    for copy in swaps[2:]:
+        copy.wait_send()
     for copy in own:
         copy.wait()
 
@@ -758,12 +785,15 @@
             pltpu.VMEM((2, ROWS * GROUP, HD), F32),
             pltpu.VMEM((LANES, HD), F32),
             pltpu.VMEM((32, 2 * ROWS, HD), BF16),
-            pltpu.VMEM((2, 2 * ROWS, HD), F32),
-            pltpu.SemaphoreType.DMA((4,)),
-            pltpu.SemaphoreType.DMA((4,)),
-            pltpu.SemaphoreType.DMA((7,)),
+            pltpu.VMEM((2, 8, ROWS, HD), BF16),
+            pltpu.VMEM((2, 2, ROWS, HD), F32),
+            pltpu.SemaphoreType.DMA((2,)),
+            pltpu.SemaphoreType.DMA((2,)),
+            pltpu.SemaphoreType.DMA((9,)),
             pltpu.SemaphoreType.DMA((32,)),
             pltpu.SemaphoreType.DMA((32,)),
+            pltpu.SemaphoreType.DMA((2, 8)),
+            pltpu.SemaphoreType.DMA((2, 8)),
         ],
         compiler_params=pltpu.CompilerParams(
             collective_id=1, has_side_effects=True, vmem_limit_bytes=60 << 20

time: 88.6 us -> 80.2 us (0.905)
  Pallas kernels: 87.7 us -> 79.3 us
    pallas_call x1, Pallas kernels: 38.7 us -> 31.2 us  [give_back(): pl.pallas_call(return_kernel, out_shape=(jax.ShapeDtypeStruct((2, ROWS *...]
where the time goes in v4:
time: 80.2 us; the launch traced here: 80 us
  Pallas kernels  79.3 us (99%)
    pallas_call x1, Pallas kernels, bring(): pl.pallas_call(bring_kernel, out_shape=(jax.ShapeDtypeStruct((4, HD, LANE...  34.7 us
    pallas_call x1, Pallas kernels, give_back(): pl.pallas_call(return_kernel, out_shape=(jax.ShapeDtypeStruct((2, ROWS *...  31.2 us
    pallas_call x1, Pallas kernels, attend(): pl.pallas_call(attend_kernel, out_shape=(jax.ShapeDtypeStruct((4, HD, LAN...  10.8 us
    pallas_call x1, Pallas kernels, finish(): pl.pallas_call(finish_kernel, out_shape=(jax.ShapeDtypeStruct((ROWS, 2 *...  2.57 us

profile of v4, /device:TPU:1, one launch (start us, length us, event | category | flops | bytes accessed | tf_op | source)
XLA Modules:
  0.0 80.0 jit_solution(14819339554267181398)
XLA Ops:
  0.6 34.7 %bring.1 = (bf16[4,128,512]{2,1,0:T(8,128)(2,1)}, bf16[4,128,512]{2,1,0:T(8,128)(2,1)}, bf16[4,512,128]{2,1,0:T(8,128)(2,1)}, bf16[4,512,128]{2,1,0:T(8,128)(2,1)}, bf16[16,2,256,128]{3,2,1,0:T(8,128)(2,1)}) custom-call(bf16[64,32,128]{2,1,0:T(8,128)(2,1)} %bitcast.10, bf16[8,32,128]{2,1,0:T(8,128)(2,1)} %bitcast.12, bf16[8,32,128]{2,1,0:T(8,128)(2,1)} %bitcast.13, ...), custom_call_target="tpu_custom_call" | custom-call | tf_op jit(solution)/shard_map/bring/pallas_call | solution.py:274
  35.3 10.8 %attend.1 = (bf16[4,128,512]{2,1,0:T(8,128)(2,1)}, f32[4,128,512]{2,1,0:T(8,128)}, bf16[16,2,4,64,128]{4,3,2,1,0:T(8,128)(2,1)}) custom-call(s32[128]{0:T(128)} %order_in.1, s32[64,128]{1,0:T(8,128)} %bitcast.17, bf16[4,128,512]{2,1,0:T(8,128)(2,1)} %get-tuple-element.19.q_cols_in, bf16[4,128,512]{2,1,0:T(8,128)(2,1)} %get-tuple-element.20.g_cols_in, ...), custom_call_target="tpu_custom_call" | custom-call | flops 6442450944 | bytes 12582912 | tf_op jit(solution)/shard_map/attend/pallas_call | solution.py:528
  46.2 31.2 %give_back.1 = (bf16[2,1024,128]{2,1,0:T(8,128)(2,1)}, f32[2,1024,128]{2,1,0:T(8,128)}, f32[2,2,128,128]{3,2,1,0:T(8,128)}) custom-call(bf16[4,128,512]{2,1,0:T(8,128)(2,1)} %get-tuple-element.24.attn_in, f32[4,128,512]{2,1,0:T(8,128)} %get-tuple-element.25.dq_in, bf16[16,2,256,128]{3,2,1,0:T(8,128)(2,1)} %bitcast.9), custom_call_target="tpu_custom_call" | custom-call | tf_op jit(solution)/shard_map/give_back/pallas_call | solution.py:771
  77.4 2.6 %finish.1 = (bf16[128,16,128]{2,1,0:T(8,128)(2,1)}, f32[128,16,128]{2,1,0:T(8,128)}, f32[256,128]{1,0:T(8,128)}, f32[256,128]{1,0:T(8,128)}) custom-call(bf16[2,1024,128]{2,1,0:T(8,128)(2,1)} %get-tuple-element.27.attn, f32[2,1024,128]{2,1,0:T(8,128)} %get-tuple-element.28.dq, f32[2,2,128,128]{3,2,1,0:T(8,128)} %get-tuple-element.29.dkv), custom_call_target="tpu_custom_call" | custom-call | bytes 4194304 | tf_op jit(solution)/shard_map/finish/pallas_call | solution.py:841

commit v5 on v3

--- a/solution.py
+++ b/solution.py
@@ -76,7 +76,11 @@
     down = where_is(x, y, lax.rem(z + NZ - 1, NZ), core)
     later = where_is(x, lax.rem(y + 1, NY), z, core)
     earlier = where_is(x, lax.rem(y + NY - 1, NY), z, core)
-    greet([peer(*p) for p in peers] + [up, down, later, earlier])
+    up_z, down_z = lax.rem(z + 1, NZ), lax.rem(z + NZ - 1, NZ)
+    later_y, earlier_y = lax.rem(y + 1, NY), lax.rem(y + NY - 1, NY)
+    corners = (where_is(x, later_y, up_z, core), where_is(x, later_y, down_z, core))
+    behind = [where_is(x, earlier_y, up_z, core), where_is(x, earlier_y, down_z, core)]
+    greet([peer(*p) for p in peers] + [up, down, later, earlier, *corners, *behind])
 
     here = pl.ds(pl.multiple_of(x * 32, 32), 32)
     copies = []
@@ -125,10 +129,11 @@
         return copy
 
     def shift(way, step, kind):
-        block = block_at(0, way, step)
+        block = block_at(0, way, min(step, 3))
         copy = send(
             ring_kv.at[block, kind], ring_kv.at[NZ + block, kind],
-            y_send.at[way, step, kind], y_recv.at[way, step, kind], later,
+            y_send.at[way, step, kind], y_recv.at[way, step, kind],
+            corners[way] if step == 4 else later,
         )
         sent.append(copy)
         return copy
@@ -223,6 +228,8 @@
                 near[way, step, kind].wait_recv()
                 if step < 3 or kind == way:
                     near[way, step + 1, kind] = hop(0, way, step + 1, kind)
+                if step == 3 and kind == way:
+                    far_shift[way, 4] = shift(way, 4, way)
                 if step == 2 or (step == 1 and kind == way):
                     far_shift[way, step, kind] = shift(way, step, kind)
         for way in range(2):
@@ -235,11 +242,6 @@
         self_shift[kind].wait_recv()
         hops[1 - kind, 1, kind] = hop(1, 1 - kind, 1, kind)
     keep(NZ + z, 1)
-    last_shift = []
-    for way in range(2):
-        near[way, 4, way].wait_recv()
-        last_shift.append(shift(way, 4, way))
-    keep(block_at(0, 0, 4), 2)
     for kind in range(2):
         for way in range(2):
             far_shift[way, 2, kind].wait_recv()
@@ -247,17 +249,19 @@
     for way in range(2):
         keep(block_at(1, way, 2), 9 + way)
     settle(0)
+    settle(1)
+    for way in range(2):
+        near[way, 4, way].wait_recv()
+    keep(block_at(0, 0, 4), 2)
     for step in (1, 3):
         for way in range(2):
             for kind in range(2):
                 arriving = far_shift if step == 1 and kind == way else hops
                 arriving[way, step, kind].wait_recv()
             keep(block_at(1, way, step), 10 + step + way)
-        if step == 1:
-            for way in range(2):
-                last_shift[way].wait_recv()
-            keep(block_at(1, 0, 4), 15)
-            settle(1)
+    for way in range(2):
+        far_shift[way, 4].wait_recv()
+    keep(block_at(1, 0, 4), 15)
     for copy in sent + relays:
         copy.wait_send()
     for copy in keeps:
@@ -308,7 +312,7 @@
 
 def attend_kernel(
     order_in, docs_in, q_cols_in, g_cols_in, q_rows_in, g_rows_in, kv_in, attn_out, dq_out, dkv,
-    order, docs, q_cols, g_cols, q_rows, g_rows, attn, dq, kv, scores, key_acc, value_acc, out_acc, tops, sums, shift, dots, grads,
+    order, docs, q_cols, g_cols, q_rows, g_rows, attn, dq, kv, scores, key_acc, value_acc, out_acc, tops, sums, shift, dots,
     pos_rows, start_rows, item_list, span_list, in_sem, out_sem,
 ):
     outer = lax.axis_index("outer")
@@ -317,14 +321,15 @@
         pltpu.make_async_copy(order_in, order, in_sem.at[0]),
         pltpu.make_async_copy(docs_in, docs, in_sem.at[1]),
         pltpu.make_async_copy(q_cols_in, q_cols, in_sem.at[2]),
-        pltpu.make_async_copy(kv_in.at[:, 0], kv.at[:, 0], in_sem.at[3]),
-        pltpu.make_async_copy(kv_in.at[:, 1], kv.at[:, 1], in_sem.at[4]),
+        pltpu.make_async_copy(kv_in.at[:, 0], kv.at[pl.ds(0, 2 * NZ), 0], in_sem.at[3]),
+        pltpu.make_async_copy(kv_in.at[:, 1], kv.at[pl.ds(0, 2 * NZ), 1], in_sem.at[4]),
         pltpu.make_async_copy(g_cols_in, g_cols, in_sem.at[5]),
         pltpu.make_async_copy(q_rows_in, q_rows, in_sem.at[6]),
         pltpu.make_async_copy(g_rows_in, g_rows, in_sem.at[7]),
     ]
     for load in loads:
         load.start()
+    kv[2 * NZ] = jnp.zeros((2, 4, SPAN, HD), BF16)
     tops[...] = jnp.full_like(tops, NEG)
     sums[...] = jnp.zeros_like(sums)
     loads[0].wait()
@@ -359,7 +364,7 @@
             for part in range(8):
                 slot = step * 8 + part
                 span = order[stored + slot]
-                entry = span * SPAN + (group * 32 + slot)
+                entry = span * (2 * SPAN) + (group * 32 + slot)
                 new = []
                 for unit in range(4):
                     span_list[counts[unit]] = entry
@@ -367,7 +372,7 @@
                     new.append(counts[unit] + jnp.where(allowed, 1, 0))
                 counts = tuple(new)
             nothing = jnp.zeros((8, SPAN, HD), F32)
-            rows = pl.ds(pl.multiple_of((group * 4 + step) * 8, 8), 8)
+            rows = pl.ds((group * 4 + step) * 8, 8)
             key_acc[rows] = nothing
             value_acc[rows] = nothing
             flat = pl.ds(pl.multiple_of(step * 32, 32), 32)
@@ -380,17 +385,16 @@
     items = jnp.int32(0)
     for unit in range(4):
         for extra in range(ITEM):
-            span_list[counts[unit] + extra] = FAR
+            span_list[counts[unit] + extra] = 2 * FAR + SLOTS
         for chunk in range(SLOTS // ITEM):
             item_list[items + chunk] = unit * 128 + chunk * ITEM
         items = items + lax.div(counts[unit] - unit * 128 + ITEM - 1, ITEM)
     blank = 3 * 128 + 72
     for extra in range(ITEM):
-        span_list[blank + extra] = FAR
+        span_list[blank + extra] = 2 * FAR + SLOTS
     for extra in range(4):
         item_list[items + extra] = blank
-    steps = lax.div(items + 1, 2)
-    long_steps = lax.div(items + 3, 4)
+    steps = lax.div(items + 3, 4)
 
     iota_keys = (
         lax.broadcasted_iota(jnp.int32, (8, 8, ROWS), 0) * 8
@@ -400,8 +404,8 @@
     def entries(item):
         first = item_list[item]
         found = [span_list[first + part] for part in range(ITEM)]
-        slots = [lax.rem(entry, SLOTS) for entry in found]
-        return lax.div(first, 128), slots, [a - b for a, b in zip(found, slots)]
+        slots = [lax.rem(entry, 2 * SPAN) for entry in found]
+        return lax.div(first, 128), slots, [lax.div(a - b, 2) for a, b in zip(found, slots)]
 
     def spans(slots, kind):
         parts = []
@@ -413,7 +417,7 @@
     loads[2].wait()
     loads[3].wait()
 
-    @functools.partial(lax.fori_loop, 0, long_steps, init_val=0)
+    @functools.partial(lax.fori_loop, 0, steps, init_val=0)
     def _(step, _):
         results = []
         for item in [4 * step + part for part in range(4)]:
@@ -440,7 +444,7 @@
         shift[unit] = jnp.broadcast_to(jnp.max(tops[unit], axis=0, keepdims=True), (8, LANES))
     loads[4].wait()
 
-    @functools.partial(lax.fori_loop, 0, long_steps, init_val=0)
+    @functools.partial(lax.fori_loop, 0, steps, init_val=0)
     def _(step, _):
         results = []
         for item in [4 * step + part for part in range(4)]:
@@ -472,38 +476,22 @@
     attn_store = pltpu.make_async_copy(attn, attn_out, out_sem.at[2 * NZ])
     attn_store.start()
 
-    def ahead(step):
-        half = lax.rem(step, 2)
-        for part in range(2):
-            unit, slots, _ = entries(2 * step + part)
-            values = spans(slots, 1)
-            for lanes in sides:
-                grads[half, part, :, lanes] = jnp.dot(
-                    values, g_cols[unit, :, lanes], preferred_element_type=F32
-                )
-
-    ahead(0)
-
     @functools.partial(lax.fori_loop, 0, steps, init_val=0)
     def _(step, _):
         results = []
-        mine = []
-        for part in range(2):
-            item = 2 * step + part
+        for item in [4 * step + part for part in range(4)]:
             unit, slots, _ = entries(item)
+            keys_t = spans(slots, 0).T
+            values = spans(slots, 1)
             probs_b = []
             score_grads = []
             for lanes in sides:
                 logits = scores[item, :, lanes].reshape(32, 8, 256)
                 probs = jnp.exp2(logits - shift[unit, :, lanes][None])
-                steep = grads[lax.rem(step, 2), part, :, lanes].reshape(32, 8, 256)
-                steep = probs * (steep - dots[unit, :, lanes][None])
+                steep = jnp.dot(values, g_cols[unit, :, lanes], preferred_element_type=F32)
+                steep = probs * (steep.reshape(32, 8, 256) - dots[unit, :, lanes][None])
                 probs_b.append(probs.reshape(256, 256).astype(BF16))
                 score_grads.append(steep.reshape(256, 256).astype(BF16))
-            mine.append((unit, slots, probs_b, score_grads))
-        ahead(step + 1)
-        for unit, slots, probs_b, score_grads in mine:
-            keys_t = spans(slots, 0).T
             probs_b = jnp.concatenate(probs_b, axis=1)
             score_grads = jnp.concatenate(score_grads, axis=1)
             to_values = jnp.dot(probs_b, g_rows[unit], preferred_element_type=F32)
@@ -512,10 +500,13 @@
             results.append((slots, unit, to_values, to_keys, to_query))
         for slots, unit, to_values, to_keys, to_query in results:
             dq[unit] += to_query
-            for part, slot in enumerate(slots):
-                rows = slice(part * SPAN, (part + 1) * SPAN)
-                key_acc[slot] += to_keys[rows]
-                value_acc[slot] += to_values[rows]
+            for acc, part in ((key_acc, to_keys), (value_acc, to_values)):
+                sums_of = [
+                    acc[slot] + part[index * SPAN : (index + 1) * SPAN]
+                    for index, slot in enumerate(slots)
+                ]
+                for slot, total in zip(slots, sums_of):
+                    acc[slot] = total
         return 0
 
     dq_store = pltpu.make_async_copy(dq, dq_out, out_sem.at[2 * NZ + 1])
@@ -551,16 +542,15 @@
             pltpu.VMEM((4, LANES, HD), BF16),
             pltpu.VMEM((4, HD, LANES), BF16),
             pltpu.VMEM((4, HD, LANES), F32),
-            pltpu.VMEM((2 * NZ, 2, 4, SPAN, HD), BF16),
+            pltpu.VMEM((2 * NZ + 1, 2, 4, SPAN, HD), BF16),
             pltpu.VMEM((4 * SLOTS // ITEM, ITEM * SPAN, LANES), F32),
-            pltpu.VMEM((SLOTS, SPAN, HD), F32),
-            pltpu.VMEM((SLOTS, SPAN, HD), F32),
+            pltpu.VMEM((SLOTS + 1, SPAN, HD), F32),
+            pltpu.VMEM((SLOTS + 1, SPAN, HD), F32),
             pltpu.VMEM((4, HD, LANES), F32),
             pltpu.VMEM((4, 8, LANES), F32),
             pltpu.VMEM((4, 8, LANES), F32),
             pltpu.VMEM((4, 8, LANES), F32),
             pltpu.VMEM((4, 8, LANES), F32),
-            pltpu.VMEM((2, 2, ITEM * SPAN, LANES), F32),
             pltpu.VMEM((4, 8, ROWS), jnp.int32),
             pltpu.VMEM((4, 8, ROWS), jnp.int32),
             pltpu.SMEM((80,), jnp.int32),

time: 88.6 us -> 78.4 us (0.88)
  Pallas kernels: 87.7 us -> 77.5 us
    pallas_call x1, Pallas kernels: 38.7 us -> 27.9 us  [give_back(): pl.pallas_call(return_kernel, out_shape=(jax.ShapeDtypeStruct((2, ROWS *...]
    pallas_call x1, Pallas kernels: 11.3 us -> 12.4 us  [attend(): pl.pallas_call(attend_kernel, out_shape=(jax.ShapeDtypeStruct((4, HD, LAN...]
where the time goes in v5:
time: 78.4 us; the launch traced here: 78.2 us
  Pallas kernels  77.5 us (99%)
    pallas_call x1, Pallas kernels, bring(): pl.pallas_call(bring_kernel, out_shape=(jax.ShapeDtypeStruct((4, HD, LANE...  34.7 us
    pallas_call x1, Pallas kernels, give_back(): pl.pallas_call(return_kernel, out_shape=(jax.ShapeDtypeStruct((2, ROWS *...  27.9 us
    pallas_call x1, Pallas kernels, attend(): pl.pallas_call(attend_kernel, out_shape=(jax.ShapeDtypeStruct((4, HD, LAN...  12.4 us
    pallas_call x1, Pallas kernels, finish(): pl.pallas_call(finish_kernel, out_shape=(jax.ShapeDtypeStruct((ROWS, 2 *...  2.57 us

profile of v5, /device:TPU:1, one launch (start us, length us, event | category | flops | bytes accessed | tf_op | source)
XLA Modules:
  0.0 78.2 jit_solution(718701410228937655)
XLA Ops:
  0.6 34.7 %bring.1 = (bf16[4,128,512]{2,1,0:T(8,128)(2,1)}, bf16[4,128,512]{2,1,0:T(8,128)(2,1)}, bf16[4,512,128]{2,1,0:T(8,128)(2,1)}, bf16[4,512,128]{2,1,0:T(8,128)(2,1)}, bf16[16,2,256,128]{3,2,1,0:T(8,128)(2,1)}) custom-call(bf16[64,32,128]{2,1,0:T(8,128)(2,1)} %bitcast.10, bf16[8,32,128]{2,1,0:T(8,128)(2,1)} %bitcast.12, bf16[8,32,128]{2,1,0:T(8,128)(2,1)} %bitcast.13, ...), custom_call_target="tpu_custom_call" | custom-call | tf_op jit(solution)/shard_map/bring/pallas_call | solution.py:274
  35.3 12.4 %attend.1 = (bf16[4,128,512]{2,1,0:T(8,128)(2,1)}, f32[4,128,512]{2,1,0:T(8,128)}, bf16[16,2,4,64,128]{4,3,2,1,0:T(8,128)(2,1)}) custom-call(s32[128]{0:T(128)} %order_in.1, s32[64,128]{1,0:T(8,128)} %bitcast.17, bf16[4,128,512]{2,1,0:T(8,128)(2,1)} %get-tuple-element.19.q_cols_in, bf16[4,128,512]{2,1,0:T(8,128)(2,1)} %get-tuple-element.20.g_cols_in, ...), custom_call_target="tpu_custom_call" | custom-call | flops 6442450944 | bytes 12582912 | tf_op jit(solution)/shard_map/attend/pallas_call | solution.py:527
  47.7 27.9 %give_back.1 = (bf16[2,1024,128]{2,1,0:T(8,128)(2,1)}, f32[2,1024,128]{2,1,0:T(8,128)}, f32[2,2,128,128]{3,2,1,0:T(8,128)}) custom-call(bf16[4,128,512]{2,1,0:T(8,128)(2,1)} %get-tuple-element.24.attn_in, f32[4,128,512]{2,1,0:T(8,128)} %get-tuple-element.25.dq_in, bf16[16,2,256,128]{3,2,1,0:T(8,128)(2,1)} %bitcast.9), custom_call_target="tpu_custom_call" | custom-call | tf_op jit(solution)/shard_map/give_back/pallas_call | solution.py:734
  75.6 2.6 %finish.1 = (bf16[128,16,128]{2,1,0:T(8,128)(2,1)}, f32[128,16,128]{2,1,0:T(8,128)}, f32[256,128]{1,0:T(8,128)}, f32[256,128]{1,0:T(8,128)}) custom-call(bf16[2,1024,128]{2,1,0:T(8,128)(2,1)} %get-tuple-element.27.attn, f32[2,1024,128]{2,1,0:T(8,128)} %get-tuple-element.28.dq, f32[2,2,128,128]{3,2,1,0:T(8,128)} %get-tuple-element.29.dkv), custom_call_target="tpu_custom_call" | custom-call | bytes 4194304 | tf_op jit(solution)/shard_map/finish/pallas_call | solution.py:801

commit v6 on v5

--- a/solution.py
+++ b/solution.py
@@ -312,7 +312,7 @@
 
 def attend_kernel(
     order_in, docs_in, q_cols_in, g_cols_in, q_rows_in, g_rows_in, kv_in, attn_out, dq_out, dkv,
-    order, docs, q_cols, g_cols, q_rows, g_rows, attn, dq, kv, scores, key_acc, value_acc, out_acc, tops, sums, shift, dots,
+    order, docs, q_cols, g_cols, q_rows, g_rows, attn, dq, dq_b, kv, scores, key_acc, value_acc, out_acc, tops, sums, shift, dots,
     pos_rows, start_rows, item_list, span_list, in_sem, out_sem,
 ):
     outer = lax.axis_index("outer")
@@ -509,7 +509,8 @@
                     acc[slot] = total
         return 0
 
-    dq_store = pltpu.make_async_copy(dq, dq_out, out_sem.at[2 * NZ + 1])
+    dq_b[...] = (dq[...] * SCALE).astype(BF16)
+    dq_store = pltpu.make_async_copy(dq_b, dq_out, out_sem.at[2 * NZ + 1])
     dq_store.start()
     stores = [attn_store, dq_store]
     for index in range(2 * NZ):
@@ -528,7 +529,7 @@
         attend_kernel,
         out_shape=(
             jax.ShapeDtypeStruct((4, HD, LANES), BF16),
-            jax.ShapeDtypeStruct((4, HD, LANES), F32),
+            jax.ShapeDtypeStruct((4, HD, LANES), BF16),
             jax.ShapeDtypeStruct((2 * NZ, 2, 4, SPAN, HD), BF16),
         ),
         in_specs=[HBM] * 7,
@@ -542,6 +543,7 @@
             pltpu.VMEM((4, LANES, HD), BF16),
             pltpu.VMEM((4, HD, LANES), BF16),
             pltpu.VMEM((4, HD, LANES), F32),
+            pltpu.VMEM((4, HD, LANES), BF16),
             pltpu.VMEM((2 * NZ + 1, 2, 4, SPAN, HD), BF16),
             pltpu.VMEM((4 * SLOTS // ITEM, ITEM * SPAN, LANES), F32),
             pltpu.VMEM((SLOTS + 1, SPAN, HD), F32),
@@ -621,16 +623,14 @@
         for half in range(2):
             unit = 2 * block + half
             rows = pl.ds(half * LANES, LANES)
-            for source, scale, target in ((attn, None, rows_tmp), (dq, SCALE, dq_rows.at[block, rows])):
+            for source, target in ((attn, attn_rows), (dq, dq_rows)):
                 for pair in range(4):
-                    tile = source[unit, :, pair * ROWS : (pair + 1) * ROWS].astype(F32)
-                    tile = tile.T if scale is None else (tile * scale).T
+                    tile = source[unit, :, pair * ROWS : (pair + 1) * ROWS].astype(F32).T
                     for part in range(2):
-                        target[pl.ds(2 * pair + part, SPAN, stride=GROUP), :] = tile[
+                        rows_tmp[pl.ds(2 * pair + part, SPAN, stride=GROUP), :] = tile[
                             part * SPAN : (part + 1) * SPAN
                         ]
-                if scale is None:
-                    attn_rows[block, rows, :] = rows_tmp[...].astype(BF16)
+                target[block, rows, :] = rows_tmp[...].astype(BF16)
 
     def swap():
         turn(1 - core)
@@ -735,17 +735,17 @@
         return_kernel,
         out_shape=(
             jax.ShapeDtypeStruct((2, ROWS * GROUP, HD), BF16),
-            jax.ShapeDtypeStruct((2, ROWS * GROUP, HD), F32),
+            jax.ShapeDtypeStruct((2, ROWS * GROUP, HD), BF16),
             jax.ShapeDtypeStruct((2, 2, ROWS, HD), F32),
         ),
         in_specs=[HBM] * 3,
         out_specs=(HBM,) * 3,
         scratch_shapes=[
             pltpu.VMEM((4, HD, LANES), BF16),
-            pltpu.VMEM((4, HD, LANES), F32),
+            pltpu.VMEM((4, HD, LANES), BF16),
             pltpu.VMEM((2 * NZ, 2, 2 * ROWS, HD), BF16),
             pltpu.VMEM((2, ROWS * GROUP, HD), BF16),
-            pltpu.VMEM((2, ROWS * GROUP, HD), F32),
+            pltpu.VMEM((2, ROWS * GROUP, HD), BF16),
             pltpu.VMEM((LANES, HD), F32),
             pltpu.VMEM((32, 2 * ROWS, HD), BF16),
             pltpu.VMEM((2, 2 * ROWS, HD), F32),
@@ -788,7 +788,7 @@
     stores.append(store)
     loads[2].wait()
     wide_joined[...] = jnp.concatenate(
-        [wide[half].reshape(ROWS, GROUP, HD) for half in range(2)], axis=1
+        [wide[half].astype(F32).reshape(ROWS, GROUP, HD) for half in range(2)], axis=1
     )
     store = pltpu.make_async_copy(wide_joined, dq_out, sem.at[3])
     store.start()
@@ -811,7 +811,7 @@
         scratch_shapes=[
             pltpu.VMEM((2, ROWS * GROUP, HD), BF16),
             pltpu.VMEM((ROWS, 2 * GROUP, HD), BF16),
-            pltpu.VMEM((2, ROWS * GROUP, HD), F32),
+            pltpu.VMEM((2, ROWS * GROUP, HD), BF16),
             pltpu.VMEM((ROWS, 2 * GROUP, HD), F32),
             pltpu.VMEM((2, 2, ROWS, HD), F32),
             pltpu.VMEM((2 * ROWS, HD), F32),

time: 78.4 us -> 78.3 us (level)
    pallas_call x1, Pallas kernels: 12.4 us -> 8.17 us  [attend(): pl.pallas_call(attend_kernel, out_shape=(jax.ShapeDtypeStruct((4, HD, LAN...]
    pallas_call x1, Pallas kernels: 27.9 us -> 32 us  [give_back(): pl.pallas_call(return_kernel, out_shape=(jax.ShapeDtypeStruct((2, ROWS *...]
where the time goes in v6:
time: 78.3 us; the launch traced here: 78 us
  Pallas kernels  77.3 us (99%)
    pallas_call x1, Pallas kernels, bring(): pl.pallas_call(bring_kernel, out_shape=(jax.ShapeDtypeStruct((4, HD, LANE...  34.7 us
    pallas_call x1, Pallas kernels, give_back(): pl.pallas_call(return_kernel, out_shape=(jax.ShapeDtypeStruct((2, ROWS *...  32 us
    pallas_call x1, Pallas kernels, attend(): pl.pallas_call(attend_kernel, out_shape=(jax.ShapeDtypeStruct((4, HD, LAN...  8.17 us
    pallas_call x1, Pallas kernels, finish(): pl.pallas_call(finish_kernel, out_shape=(jax.ShapeDtypeStruct((ROWS, 2 *...  2.42 us

profile of v6, /device:TPU:1, one launch (start us, length us, event | category | flops | bytes accessed | tf_op | source)
XLA Modules:
  0.0 78.0 jit_solution(2111095987806708380)
XLA Ops:
  0.6 34.7 %bring.1 = (bf16[4,128,512]{2,1,0:T(8,128)(2,1)}, bf16[4,128,512]{2,1,0:T(8,128)(2,1)}, bf16[4,512,128]{2,1,0:T(8,128)(2,1)}, bf16[4,512,128]{2,1,0:T(8,128)(2,1)}, bf16[16,2,256,128]{3,2,1,0:T(8,128)(2,1)}) custom-call(bf16[64,32,128]{2,1,0:T(8,128)(2,1)} %bitcast.10, bf16[8,32,128]{2,1,0:T(8,128)(2,1)} %bitcast.12, bf16[8,32,128]{2,1,0:T(8,128)(2,1)} %bitcast.13, ...), custom_call_target="tpu_custom_call" | custom-call | tf_op jit(solution)/shard_map/bring/pallas_call | solution.py:274
  35.3 8.2 %attend.1 = (bf16[4,128,512]{2,1,0:T(8,128)(2,1)}, bf16[4,128,512]{2,1,0:T(8,128)(2,1)}, bf16[16,2,4,64,128]{4,3,2,1,0:T(8,128)(2,1)}) custom-call(s32[128]{0:T(128)} %order_in.1, s32[64,128]{1,0:T(8,128)} %bitcast.17, bf16[4,128,512]{2,1,0:T(8,128)(2,1)} %get-tuple-element.19.q_cols_in, bf16[4,128,512]{2,1,0:T(8,128)(2,1)} %get-tuple-element.20.g_cols_in, ...), custom_call_target="tpu_custom_call" | custom-call | flops 6442450944 | bytes 12582912 | tf_op jit(solution)/shard_map/attend/pallas_call | solution.py:528
  43.5 32.0 %give_back.1 = (bf16[2,1024,128]{2,1,0:T(8,128)(2,1)}, bf16[2,1024,128]{2,1,0:T(8,128)(2,1)}, f32[2,2,128,128]{3,2,1,0:T(8,128)}) custom-call(bf16[4,128,512]{2,1,0:T(8,128)(2,1)} %get-tuple-element.24.attn_in, bf16[4,128,512]{2,1,0:T(8,128)(2,1)} %get-tuple-element.25.dq_in, bf16[16,2,256,128]{3,2,1,0:T(8,128)(2,1)} %bitcast.9), custom_call_target="tpu_custom_call" | custom-call | tf_op jit(solution)/shard_map/give_back/pallas_call | solution.py:734
  75.5 2.4 %finish.1 = (bf16[128,16,128]{2,1,0:T(8,128)(2,1)}, f32[128,16,128]{2,1,0:T(8,128)}, f32[256,128]{1,0:T(8,128)}, f32[256,128]{1,0:T(8,128)}) custom-call(bf16[2,1024,128]{2,1,0:T(8,128)(2,1)} %get-tuple-element.27.attn, bf16[2,1024,128]{2,1,0:T(8,128)(2,1)} %get-tuple-element.28.dq, f32[2,2,128,128]{3,2,1,0:T(8,128)} %get-tuple-element.29.dkv), custom_call_target="tpu_custom_call" | custom-call | bytes 4194304 | tf_op jit(solution)/shard_map/finish/pallas_call | solution.py:801
